TPU v7x, 256 devices: a whole 4x4x8 slice. The times are simulated.
256 devices in a mesh: dp: 8 (over y, core), mp: 32 (over z, x).
Axes of the slice: x: 4, y: 4, z: 8, core: 2. Of those that a mesh axis runs over, the one named last changes fastest.
Arguments:
- gradient: bfloat16 [12288, 28672], P('dp', 'mp'), as said below
- owners: int32 [32, 1], replicated, may hold values from 0 to 7, as said below
- left_old: float32 [24, 512, 512], P('dp', 'mp'), may hold values from -3 to 3
- right_old: float32 [48, 896, 896], P('dp', 'mp'), may hold values from -3 to 3
Outputs:
- left_stats: float32 [24, 512, 512], P('dp', 'mp')
- right_stats: float32 [48, 896, 896], P('dp', 'mp')
Inputs may be any that keep to these rules, and one draw needn't show every extreme that they name: `owners`: each owner holds at most 6 and at least 2 blocks of the whole gradient; some owner holds exactly 6 and another exactly 2. `gradient`: finite values of order one or smaller.
All inputs are finite; a program needn't handle non-finite values.
Results may differ from a plain program's by a relative error of at most 0.0003.
Values sent between devices are 32-bit elements; how exact they have to be, the bound alone decides.
A program may use at most 64 MiB of HBM per device.

v0:
```python
import jax
import jax.numpy as jnp
from jax import lax
from jax.sharding import PartitionSpec as P

RB = 896


BETA = 0.95


def per_device(gradient, owners, left_old, right_old):
    row_count, col_count = gradient.shape
    left_count = left_old.shape[0]
    left_width = left_old.shape[2]
    grad_blocks = gradient.reshape(left_count, left_width, col_count)
    mine_rows = lax.psum_scatter(
        jnp.einsum("lrc,lsc->rls", grad_blocks, grad_blocks, preferred_element_type=jnp.float32),
        "mp",
        scatter_dimension=0,
        tiled=True,
    )
    left_stats = BETA * left_old + jnp.transpose(mine_rows, (1, 0, 2))
    block_count = col_count // RB
    capacity = right_old.shape[0]
    grad_cols = gradient.reshape(row_count, block_count, RB)
    partial_gram = jnp.einsum(
        "rjc,rjd->jcd", grad_cols, grad_cols, preferred_element_type=jnp.float32
    )
    all_owners = owners[:, 0]
    total_blocks = all_owners.shape[0]
    same_owner = all_owners[:, None] == all_owners[None, :]
    block_range = jnp.arange(total_blocks, dtype=jnp.int32)
    earlier = block_range[None, :] < block_range[:, None]
    owner_rank = jnp.sum((same_owner & earlier).astype(jnp.int32), axis=1)
    slot_range = jnp.arange(capacity, dtype=jnp.int32)
    data_index = lax.axis_index("dp")
    select_mine = (
        (all_owners[None, :] == data_index) & (owner_rank[None, :] == slot_range[:, None])
    ).astype(jnp.float32)
    valid = jnp.sum(select_mine, axis=1)
    summed_blocks = lax.psum(partial_gram, "dp")
    pieces = lax.all_to_all(summed_blocks, "mp", split_axis=1, concat_axis=0, tiled=True)
    fresh_right = jnp.einsum("kb,bad->kad", select_mine, pieces, precision=lax.Precision.HIGHEST)
    right_stats = BETA * valid[:, None, None] * right_old + fresh_right
    return (left_stats, right_stats)


def solution(mesh):
    in_specs = (P("dp", "mp"), P(), P("dp", "mp", None), P("dp", "mp", None))
    out_specs = (P("dp", "mp", None), P("dp", "mp", None))
    return jax.shard_map(
        per_device, mesh=mesh, in_specs=in_specs, out_specs=out_specs, check_vma=False
    )
```

profile of v0, /device:TPU:1, one launch (start us, length us, event | category | flops | bytes accessed | tf_op | source)
XLA Modules:
  0.0 353.8 jit_solution(5996245873807949179)
XLA Ops:
  8.0 0.0 copy-start
  8.0 0.0 all-reduce.4.cloned.1.call-start
  8.1 1.7 copy-done
  9.8 4.7 %convolution_bitcast_fusion = f32[1,896,896]{2,1,0:T(8,128)} fusion(bf16[1536,896]{1,0:T(8,128)(2,1)S(1)} %copy-done), kind=kOutput, calls=%fused_computation.2 | convolution fusion | flops 2466250752 | bytes 5963776 | tf_op jit(solution)/shard_map/rjc,rjd->jcd/dot_general | solution.py:27
  14.5 0.0 all-reduce.4.cloned.1.call-update
  14.5 76.5 %all-reduce.4.cloned.1.call-done = f32[1,896,896]{2,1,0:T(8,128)} async-done(((f32[1,896,896]{2,1,0:T(8,128)}), f32[1,896,896]{2,1,0:T(8,128)}) %all-reduce.4.cloned.1.call-update) | async-done | bytes 3211280 | tf_op jit(solution)/shard_map/psum | solution.py:42
  91.1 7.0 %copy.28 = f32[1,896,896]{2,0,1:T(1,128)} copy(f32[1,896,896]{2,1,0:T(8,128)} %all-reduce.4.cloned.1.call-done) | data formatting | bytes 6422528 | tf_op jit(solution)/shard_map/psum | solution.py:42
  98.0 9.6 %all-to-all-start = ((f32[1,896,896]{2,0,1:T(1,128)}), f32[1,896,896]{2,0,1:T(1,128)}, u32[]{:S(2)}, u32[]{:S(2)}) async-start(f32[1,896,896]{2,0,1:T(1,128)} %copy.28), calls=%async_computation | async-start | bytes 6422528 | tf_op jit(solution)/shard_map/all_to_all | solution.py:43
  107.7 0.2 all-reduce.6.cloned.1.call-start
  107.9 3.5 convolution_bitcast_fusion.1
  111.4 5.1 %copy.26 = f32[512,3,512]{2,1,0:T(4,128)} copy(f32[512,3,512]{0,2,1:T(8,128)} %convolution_bitcast_fusion.1) | data formatting | bytes 6291456 | tf_op jit(solution)/shard_map/lrc,lsc->rls/transpose | solution.py:18
  116.5 0.0 copy-start.4
  116.5 0.0 copy-start.3
  116.5 0.0 copy-start.2
  116.5 0.0 all-reduce.6.cloned.1.call-update
  116.6 0.6 copy-done.4
  117.2 0.6 dynamic-slice
  118.5 0.0 copy-done.3
  118.5 0.2 convert_reduce_fusion
  118.7 0.1 convert_reduce_fusion.1
  118.8 204.0 %all-reduce.6.cloned.1.call-done = f32[512,3,512]{2,1,0:T(4,128)} async-done(((f32[512,3,512]{2,1,0:T(4,128)}), f32[512,3,512]{2,1,0:T(4,128)}) %all-reduce.6.cloned.1.call-update) | async-done | bytes 3145744
  322.8 0.0 copy-done.2
  322.8 1.0 fusion.5
  323.8 0.7 copy.30
  324.4 0.0 all-to-all-done
  324.4 11.2 %reduce = f32[896,896]{1,0:T(8,128)} reduce(f32[1,896,896]{2,0,1:T(1,128)} %all-to-all-done, f32[]{:T(128)} %constant.19), dimensions={0}, to_apply=%all_to_all.4.reduce_sub_computation | reduce | bytes 6422532 | tf_op jit(solution)/shard_map/all_to_all | solution.py:43
  335.7 0.0 copy-start.1
  335.7 4.6 %all_to_all.10 = f32[32,28,896]{2,1,0:T(8,128)} reshape(f32[896,896]{1,0:T(8,128)} %reduce) | data formatting | bytes 6422528 | tf_op jit(solution)/shard_map/all_to_all | solution.py:43
  340.3 0.0 copy-done.1
  340.3 5.1 %fusion.2 = f32[6,28,896]{2,0,1:T(8,128)S(1)} fusion(f32[32,28,896]{2,1,0:T(8,128)} %all_to_all.10, f32[6,28,896]{2,1,0:T(8,128)S(1)} %copy-done.1, f32[6]{0:T(128)S(1)} %broadcast_multiply_fusion, s32[32]{0:T(128)S(1)} %convert_reduce_fusion, pred[32]{0:T(512)(128)(4,1)S(1)} %broadcast_compare_fusion), kind=kOutput, calls=%fused_computation.4 | convolution fusion | flops 58104192 | bytes 4415672 | tf_op jit(solution)/shard_map/kb,bad->kad/dot_general | solution.py:44
  345.4 1.0 copy.31
  (2 shorter events, 0.0 us)
Async XLA Ops:
  8.0 1.8 copy-start
  8.0 83.1 %all-reduce.4.cloned.1.call-start = ((), (), s32[]{:S(2)}) async-start(), calls=%async_computation.1 | async-start | bytes 6422528 | tf_op jit(solution)/shard_map/psum | solution.py:42
  98.0 226.4 %all-to-all-start = ((f32[1,896,896]{2,0,1:T(1,128)}), f32[1,896,896]{2,0,1:T(1,128)}, u32[]{:S(2)}, u32[]{:S(2)}) async-start(f32[1,896,896]{2,0,1:T(1,128)} %copy.28), calls=%async_computation | async-start | bytes 6422528 | tf_op jit(solution)/shard_map/all_to_all | solution.py:43
  107.7 215.0 %all-reduce.6.cloned.1.call-start = ((), (), s32[]{:S(2)}) async-start(), calls=%async_computation.2 | async-start | bytes 8388608
  116.5 0.7 copy-start.4
  116.5 1.9 copy-start.3
  116.5 206.2 %copy-start.2 = (f32[3,16,512]{2,1,0:T(8,128)S(1)}, f32[3,16,512]{2,1,0:T(8,128)}, u32[]{:S(2)}) copy-start(f32[3,16,512]{2,1,0:T(8,128)} %param.6) | copy-start | bytes 294916
  335.7 4.6 %copy-start.1 = (f32[6,28,896]{2,1,0:T(8,128)S(1)}, f32[6,28,896]{2,1,0:T(8,128)}, u32[]{:S(2)}) copy-start(f32[6,28,896]{2,1,0:T(8,128)} %param.7) | copy-start | bytes 1806340
Sparse Core Ops, SparseCore 0:
  14.7 76.3 all-reduce.3
Sparse Core Ops, SparseCore 1:
  116.7 206.0 all-reduce.5
where the time goes:
time: 357 us; the launch traced here: 354 us
  waiting for transfers between devices  281 us (79%)
  local copies, waits for them, and re-layouts  21.3 us (6%)
  between operations  16.2 us (5%)
  matrix products  13.4 us (4%)
  other arithmetic  12.6 us (4%)
  starting transfers between devices  9.91 us (3%)
    unnamed x3, waiting for transfers between devices  204 us
    psum x1, waiting for transfers between devices, per_device(): summed_blocks = lax.psum(partial_gram, 'dp')  76.5 us
    all_to_all x1, other arithmetic, per_device(): lax.all_to_all(summed_blocks, 'mp', split_axis=1, concat_axis=0, tiled=True)  11.2 us
    all_to_all x1, starting transfers between devices, per_device(): lax.all_to_all(summed_blocks, 'mp', split_axis=1, concat_axis=0, tiled=True)  9.65 us
  transfers between devices with their start and end apart: 3, of which 2 were waited for; matrix products, arithmetic and copies ran while one was open for 3% of the time, Pallas kernels for 0%

commit v1 on v0

v1 whole, which is shorter than its diff:
```python
import functools

import jax
import jax.numpy as jnp
from jax import lax
from jax.experimental import pallas as pl
from jax.experimental.pallas import tpu as pltpu
from jax.sharding import PartitionSpec as P

BETA = 0.95
F32 = jnp.float32
BF16 = jnp.bfloat16
RB = 896
T = 128
NT = 7
NMP = 32
NDP = 8
CAP = 6
RPM = 28
NY = 4
NX = 4
NZ = 8


def remote(src, dst, send_sem, recv_sem, dp, mp):
    return pltpu.make_async_remote_copy(
        src_ref=src,
        dst_ref=dst,
        send_sem=send_sem,
        recv_sem=recv_sem,
        device_id=(dp, mp),
        device_id_type=pl.DeviceIdType.MESH,
    )


def kernel(
    grad_ref, grad5_ref, table_ref, left_ref, right_ref,
    h, ht, a, part, ra, rb1, rb2, s2, r2, s3, r3,
    lp, lx1, lx2, lz, lzr, lt,
    in_sem, ra_send, ra_recv, rb_send, rb_recv, r2_send, r2_recv, r3_send, r3_recv,
    lx_send, lx_recv, lz_send, lz_recv, lt_sem,
):
    dp = lax.axis_index("dp")
    mp = lax.axis_index("mp")
    y, c = dp // 2, dp % 2
    z, x = mp // NX, mp % NX
    other = 1 - c

    load_h = pltpu.make_async_copy(grad_ref, h.at[:, pl.ds(0, RB)], in_sem.at[0])
    load_h.start()
    load_a = []
    for j in range(6):
        cp = pltpu.make_async_copy(grad5_ref.at[:, :, (x + j) % NX], a.at[j], in_sem.at[1 + j])
        cp.start()
        load_a.append(cp)

    barrier = pltpu.get_barrier_semaphore()

    def hello_mp(i, carry):
        pl.semaphore_signal(barrier, inc=1, device_id=(dp, (mp + i) % NMP), device_id_type=pl.DeviceIdType.MESH)
        return carry

    def hello_dp(i, carry):
        pl.semaphore_signal(barrier, inc=1, device_id=((dp + i) % NDP, mp), device_id_type=pl.DeviceIdType.MESH)
        return carry

    lax.fori_loop(1, NDP, hello_dp, 0)
    lax.fori_loop(1, NMP, hello_mp, 0)

    h[:, pl.ds(RB, T)] = jnp.zeros((h.shape[0], T), BF16)
    load_h.wait()
    for t in range(NT):
        ht[t * T:(t + 1) * T, :] = h[:, t * T:(t + 1) * T].T

    pl.semaphore_wait(barrier, NMP - 1 + NDP - 1)

    def has(q, core):
        return 2 * q + core < NT

    order = [(y + k) % NY for k in (2, 1, 3, 0)]

    def ra_copy(q, i):
        return remote(part.at[2 * q + other], ra.at[q], ra_send.at[i], ra_recv.at[i], dp + 1 - 2 * c, mp)

    for i, q in enumerate(order):
        cols = pl.ds(pl.multiple_of(q * 2 * T, 2 * T), 2 * T)
        block = jnp.dot(ht[...], h[:, cols], preferred_element_type=F32)
        part[2 * q] = block[:, :T]
        part[2 * q + 1] = block[:, T:]

        @pl.when(has(q, other))
        def _():
            ra_copy(q, i).start()

    for cp in load_a:
        cp.wait()

    def left_part(j):
        for l in range(3):
            rows = a[j, l].reshape(T, RB)
            cols = a[j:j + 3, l].reshape(3 * T, RB)
            lp[j, l] = lax.dot_general(rows, cols, (((1,), (1,)), ((), ())), preferred_element_type=F32)

    half = T // 2
    xr = z * NX + (x + 1) % NX
    xl = z * NX + (x + 3) % NX
    left_part(2)
    lx1_r = remote(lp.at[2, :, pl.ds(0, half)], lx1.at[0], lx_send.at[0], lx_recv.at[0], dp, xr)
    lx1_l = remote(lp.at[2, :, pl.ds(half, half)], lx1.at[1], lx_send.at[1], lx_recv.at[1], dp, xl)
    lx1_r.start()
    lx1_l.start()

    yr = 2 * ((y + 1) % NY) + c
    yl = 2 * ((y + 3) % NY) + c
    hr = RB // 2

    def ra_sum(i):
        q = order[i]

        @pl.when(has(q, c))
        def _():
            ra_copy(q, i).wait_recv()
            part[2 * q + c] = part[2 * q + c] + ra[q]

    q2, q1, q3, q0 = order
    ra_sum(0)
    rb1_r = remote(part.at[2 * q2 + c, pl.ds(0, hr)], rb1.at[0], rb_send.at[0], rb_recv.at[0], yr, mp)
    rb1_l = remote(part.at[2 * q2 + c, pl.ds(hr, hr)], rb1.at[1], rb_send.at[1], rb_recv.at[1], yl, mp)

    @pl.when(has(q2, c))
    def _():
        rb1_r.start()
        rb1_l.start()

    left_part(1)
    left_part(3)
    ra_sum(1)
    ra_sum(2)

    rb2_r = remote(part.at[2 * q1 + c], rb2.at[0], rb_send.at[2], rb_recv.at[2], yr, mp)
    rb2_l = remote(part.at[2 * q3 + c], rb2.at[1], rb_send.at[3], rb_recv.at[3], yl, mp)

    @pl.when(has(q1, c))
    def _():
        rb1_r.wait_recv()
        part[2 * q1 + c, :hr] = part[2 * q1 + c, :hr] + rb1[0]
        rb2_r.start()

    @pl.when(has(q3, c))
    def _():
        rb1_l.wait_recv()
        part[2 * q3 + c, hr:] = part[2 * q3 + c, hr:] + rb1[1]
        rb2_l.start()

    lx1_r.wait_recv()
    lp[1, :, :half] = lp[1, :, :half] + lx1[0]
    lx2_r = remote(lp.at[1], lx2.at[0], lx_send.at[2], lx_recv.at[2], dp, xr)
    lx2_r.start()
    lx1_l.wait_recv()
    lp[3, :, half:] = lp[3, :, half:] + lx1[1]
    lx2_l = remote(lp.at[3], lx2.at[1], lx_send.at[3], lx_recv.at[3], dp, xl)
    lx2_l.start()
    left_part(0)

    ra_sum(3)
    active = dp < NT

    def r2_copy(i):
        return remote(s2.at[(mp + i) % NMP], r2.at[NMP - i], r2_send, r2_recv, dp, (mp + i) % NMP)

    @pl.when(active)
    def _():
        rb2_r.wait_recv()
        rb2_l.wait_recv()
        part[dp] = part[dp] + rb2[0] + rb2[1]
        for m in range(NMP):
            s2[m] = part[dp, RPM * m:RPM * (m + 1)]

        def go(i, carry):
            r2_copy(i).start()
            return carry

        lax.fori_loop(1, NMP, go, 0)
        r2[0] = s2[mp]

    lx2_r.wait_recv()
    lx2_l.wait_recv()
    for l in range(3):
        band = lp[0, l] + lx2[0, l] + lx2[1, l]
        lz[:, l, :, :3 * T] = band.reshape(NZ, 16, 3 * T)
        lz[:, l, :, 3 * T:] = band[:, T:2 * T].T.reshape(NZ, 16, T)

    zr = ((z + 1) % NZ) * NX + x
    zl = ((z + NZ - 1) % NZ) * NX + x
    hc = 2 * T

    def lz_copies(s):
        to_r = (z + 5 - s) % NZ
        to_l = (z + NZ - 5 + s) % NZ
        if s == 1:
            src_r, dst_r = lz.at[to_r, :, :, pl.ds(0, hc)], lzr.at[0, 0, :, :, pl.ds(0, hc)]
            src_l, dst_l = lz.at[to_l, :, :, pl.ds(hc, hc)], lzr.at[1, 0, :, :, pl.ds(hc, hc)]
        else:
            src_r, dst_r = lz.at[to_r], lzr.at[0, s - 1]
            src_l, dst_l = lz.at[to_l], lzr.at[1, s - 1]
        return (
            remote(src_r, dst_r, lz_send.at[0, s - 1], lz_recv.at[0, s - 1], dp, zr),
            remote(src_l, dst_l, lz_send.at[1, s - 1], lz_recv.at[1, s - 1], dp, zl),
        )

    lz_all = [lz_copies(s) for s in (1, 2, 3, 4)]

    def lz_start(s):
        for cp in lz_all[s - 1]:
            cp.start()

    def lz_take(s):
        r, l = lz_all[s - 1]
        near = (z + 4 - s) % NZ
        r.wait_recv()
        if s == 1:
            lz[near, :, :, :hc] = lz[near, :, :, :hc] + lzr[0, 0, :, :, :hc]
        else:
            lz[near] = lz[near] + lzr[0, s - 1]
        far = (z + NZ - 4 + s) % NZ
        l.wait_recv()
        if s == 1:
            lz[far, :, :, hc:] = lz[far, :, :, hc:] + lzr[1, 0, :, :, hc:]
        else:
            lz[far] = lz[far] + lzr[1, s - 1]

    lz_start(1)
    lz_take(1)
    lz_start(2)

    def r3_copy(i):
        o = (dp + i) % NDP
        return remote(s3.at[o], r3.at[dp], r3_send.at[i], r3_recv.at[dp], o, mp)

    @pl.when(active)
    def _():
        everything = r2.at[pl.ds(1, NMP - 1)]
        pltpu.make_async_copy(everything, everything, r2_recv).wait()
        for o in range(NDP):
            for k in range(CAP):
                s3[o, RPM * k:RPM * (k + 1), :] = r2[table_ref[o * CAP + k]]
        for i in range(1, NDP):
            r3_copy(i).start()
        r3[dp] = s3[dp]

    for s in (2, 3):
        lz_take(s)
        lz_start(s + 1)
    lz_take(4)
    last = remote(lz.at[z, :, :, pl.ds(3 * T, T)], lt, lt_sem.at[0], lt_sem.at[1], dp, xr)
    last.start()

    p = lax.broadcasted_iota(jnp.int32, (NX * T, NX * T), 0)
    q = lax.broadcasted_iota(jnp.int32, (NX * T, NX * T), 1)
    place = ((p // 16) % NZ) * (16 * NX) + ((p // T + x) % NX) * 16 + p % 16
    perm = (place == q).astype(F32)
    last.wait_recv()
    for l in range(3):
        row = jnp.concatenate([lz[z, l, :, :3 * T], lt[l]], axis=1)
        left_ref[l] = jnp.dot(row, perm, precision=lax.Precision.HIGHEST, preferred_element_type=F32)

    for d in range(NT):
        @pl.when(dp != d)
        def _():
            pltpu.make_async_copy(r3.at[d], r3.at[d], r3_recv.at[d]).wait()

        for k in range(CAP):
            right_ref[k, :, d * T:(d + 1) * T] = r3[d, RPM * k:RPM * (k + 1), :]

    for i, q_ in enumerate(order):
        @pl.when(has(q_, other))
        def _():
            ra_copy(q_, i).wait_send()

    @pl.when(has(q2, c))
    def _():
        rb1_r.wait_send()
        rb1_l.wait_send()

    @pl.when(has(q1, c))
    def _():
        rb2_r.wait_send()

    @pl.when(has(q3, c))
    def _():
        rb2_l.wait_send()

    for cp in (lx1_r, lx1_l, lx2_r, lx2_l, last):
        cp.wait_send()
    for pair in lz_all:
        for cp in pair:
            cp.wait_send()

    @pl.when(active)
    def _():
        sent = s2.at[pl.ds(1, NMP - 1)]
        pltpu.make_async_copy(sent, sent, r2_send).wait()
        for i in range(1, NDP):
            r3_copy(i).wait_send()


def per_device(gradient, owners, left_old, right_old):
    rows = gradient.shape[0]
    all_owners = owners[:, 0]
    same_owner = all_owners[:, None] == all_owners[None, :]
    block = jnp.arange(NMP, dtype=jnp.int32)
    rank = jnp.sum((same_owner & (block[None, :] < block[:, None])).astype(jnp.int32), axis=1)
    place = all_owners * CAP + rank
    hit = place[None, :] == jnp.arange(NDP * CAP, dtype=jnp.int32)[:, None]
    source = jnp.sum(jnp.where(hit, block[None, :], 0), axis=1)
    table = (source - lax.axis_index("mp") + NMP) % NMP
    slot = jnp.arange(CAP, dtype=jnp.int32) + lax.axis_index("dp") * CAP
    valid = jnp.any(place[None, :] == slot[:, None], axis=1)

    left_gram, right_gram = pl.pallas_call(
        kernel,
        out_shape=(
            jax.ShapeDtypeStruct((3, 16, 512), F32),
            jax.ShapeDtypeStruct((CAP, RPM, RB), F32),
        ),
        in_specs=[
            pl.BlockSpec(memory_space=pl.ANY),
            pl.BlockSpec(memory_space=pl.ANY),
            pl.BlockSpec(memory_space=pltpu.SMEM),
        ],
        out_specs=(
            pl.BlockSpec(memory_space=pltpu.VMEM),
            pl.BlockSpec(memory_space=pltpu.VMEM),
        ),
        scratch_shapes=[
            pltpu.VMEM((rows, 1024), BF16),
            pltpu.VMEM((RB, rows), BF16),
            pltpu.VMEM((6, 3, NZ, 16, RB), BF16),
            pltpu.VMEM((8, RB, T), F32),
            pltpu.VMEM((NY, RB, T), F32),
            pltpu.VMEM((2, RB // 2, T), F32),
            pltpu.VMEM((2, RB, T), F32),
            pltpu.VMEM((NMP, RPM, T), F32),
            pltpu.VMEM((NMP, RPM, T), F32),
            pltpu.VMEM((NDP, CAP * RPM, T), F32),
            pltpu.VMEM((NDP, CAP * RPM, T), F32),
            pltpu.VMEM((NX, 3, T, 3 * T), F32),
            pltpu.VMEM((2, 3, T // 2, 3 * T), F32),
            pltpu.VMEM((2, 3, T, 3 * T), F32),
            pltpu.VMEM((NZ, 3, 16, 4 * T), F32),
            pltpu.VMEM((2, 4, 3, 16, 4 * T), F32),
            pltpu.VMEM((3, 16, T), F32),
            pltpu.SemaphoreType.DMA((7,)),
            pltpu.SemaphoreType.DMA((NY,)),
            pltpu.SemaphoreType.DMA((NY,)),
            pltpu.SemaphoreType.DMA((4,)),
            pltpu.SemaphoreType.DMA((4,)),
            pltpu.SemaphoreType.DMA,
            pltpu.SemaphoreType.DMA,
            pltpu.SemaphoreType.DMA((NDP,)),
            pltpu.SemaphoreType.DMA((NDP,)),
            pltpu.SemaphoreType.DMA((4,)),
            pltpu.SemaphoreType.DMA((4,)),
            pltpu.SemaphoreType.DMA((2, 4)),
            pltpu.SemaphoreType.DMA((2, 4)),
            pltpu.SemaphoreType.DMA((2,)),
        ],
        compiler_params=pltpu.CompilerParams(
            collective_id=0, has_side_effects=True, vmem_limit_bytes=48 * 1024 * 1024
        ),
        name="stats",
    )(gradient, gradient.reshape(3, NZ, NX, 16, RB), table)
    left_stats = BETA * left_old + left_gram
    right_stats = jnp.where(valid[:, None, None], BETA * right_old + right_gram, 0.0)
    return left_stats, right_stats


def solution(mesh):
    in_specs = (P("dp", "mp"), P(), P("dp", "mp", None), P("dp", "mp", None))
    out_specs = (P("dp", "mp", None), P("dp", "mp", None))
    return jax.shard_map(
        per_device, mesh=mesh, in_specs=in_specs, out_specs=out_specs, check_vma=False
    )
```

time: 357 us -> 73.6 us (0.21)
  the two profiles are of different devices: /device:TPU:1 before, /device:TPU:8 now
where the time goes in v1:
time: 73.6 us; the launch traced here: 73.5 us
  Pallas kernels  67.5 us (92%)
  other arithmetic  3.5 us (5%)
  local copies, waits for them, and re-layouts  1.78 us (2%)
    pallas_call x1, Pallas kernels, per_device(): pl.pallas_call(kernel, out_shape=(jax.ShapeDtypeStruct((3, 16, 512), F32)...  67.5 us
    unnamed x6, local copies, waits for them, and re-layouts  1.78 us

profile of v1, /device:TPU:8, one launch (start us, length us, event | category | flops | bytes accessed | tf_op | source)
XLA Modules:
  0.0 73.5 jit_solution(3163631312498202919)
XLA Ops:
  0.6 0.9 %convert_reduce_fusion = s32[32]{0:T(128)S(1)} fusion(s32[32]{0:T(128)} %bitcast.4), kind=kLoop, calls=%fused_computation.4 | loop fusion | flops 5088 | bytes 256 | tf_op jit(solution)/shard_map/reduce_sum | solution.py:312
  1.6 0.7 multiply_add_fusion.1
  2.2 0.2 compare_reduce_fusion
  2.4 0.1 select_reduce_fusion
  2.5 0.0 copy-start
  2.5 1.8 %copy-done = bf16[1536,896]{1,0:T(8,128)(2,1)S(1)} copy-done((bf16[1536,896]{1,0:T(8,128)(2,1)S(1)}, bf16[1536,896]{1,0:T(8,128)(2,1)}, u32[]{:S(2)}) %copy-start) | copy-done | bytes 2752536
  4.3 0.0 copy-start.2
  4.3 0.0 copy-start.1
  4.3 67.5 %stats.1 = (f32[3,16,512]{2,1,0:T(8,128)S(1)}, f32[6,28,896]{2,1,0:T(8,128)S(1)}) custom-call(bf16[1536,896]{1,0:T(8,128)(2,1)S(1)} %copy-done, bf16[3,8,4,16,896]{4,3,2,1,0:T(8,128)(2,1)S(1)} %bitcast.3, s32[48]{0:T(128)S(1)} %and_select_fusion.table_ref), custom_call_target="tpu_custom_call" | custom-call | tf_op jit(solution)/shard_map/stats/pallas_call | solution.py:320
  71.8 0.0 copy-done.2
  71.8 0.7 multiply_add_fusion
  72.5 0.0 copy-done.1
  72.5 1.0 %add_select_fusion = f32[6,28,896]{2,1,0:T(8,128)} fusion(f32[6,28,896]{2,1,0:T(8,128)S(1)} %get-tuple-element.5, f32[6,28,896]{2,1,0:T(8,128)S(1)} %copy-done.1, pred[6]{0:T(512)(128)(4,1)S(1)} %compare_reduce_fusion), kind=kLoop, calls=%fused_computation | loop fusion | flops 451584 | bytes 1806342 | tf_op jit(solution)/shard_map/jit(_where)/select_n | solution.py:374
  (2 shorter events, 0.0 us)
Async XLA Ops:
  2.5 1.8 %copy-start = (bf16[1536,896]{1,0:T(8,128)(2,1)S(1)}, bf16[1536,896]{1,0:T(8,128)(2,1)}, u32[]{:S(2)}) copy-start(bf16[1536,896]{1,0:T(8,128)(2,1)} %grad_ref.1) | copy-start | bytes 8257540
  4.3 67.5 %copy-start.2 = (f32[3,16,512]{2,1,0:T(8,128)S(1)}, f32[3,16,512]{2,1,0:T(8,128)}, u32[]{:S(2)}) copy-start(f32[3,16,512]{2,1,0:T(8,128)} %param.6) | copy-start | bytes 294916
  4.3 68.2 %copy-start.1 = (f32[6,28,896]{2,1,0:T(8,128)S(1)}, f32[6,28,896]{2,1,0:T(8,128)}, u32[]{:S(2)}) copy-start(f32[6,28,896]{2,1,0:T(8,128)} %param.7) | copy-start | bytes 1806340

commit v2 on v0

v2 whole, which is shorter than its diff:
```python
import functools

import jax
import jax.numpy as jnp
from jax import lax
from jax.experimental import pallas as pl
from jax.experimental.pallas import tpu as pltpu
from jax.sharding import PartitionSpec as P

BETA = 0.95
F32 = jnp.float32
BF16 = jnp.bfloat16
RB = 896
T = 128
NT = 7
NMP = 32
NDP = 8
CAP = 6
RPM = 28
NY = 4
NX = 4
NZ = 8


def remote(src, dst, send_sem, recv_sem, dp, mp):
    return pltpu.make_async_remote_copy(
        src_ref=src,
        dst_ref=dst,
        send_sem=send_sem,
        recv_sem=recv_sem,
        device_id=(dp, mp),
        device_id_type=pl.DeviceIdType.MESH,
    )


def kernel(
    grad_ref, grad5_ref, owners_ref, left_ref, right_ref, scale_ref,
    h, a, pb, part, ra, rb1, rb2, r2a, r2b, s3a, s3b, r3a, r3b,
    lp, lx1, lx2, lz, rly, rlyh, fin, fint, perm, tabv, tab,
    in_sem, tab_sem, ra_send, ra_recv, rb1_send, rb1_recv, rb2_send, rb2_recv,
    r2_send, r2_recv, r3_send, r3_recv,
    lx1_send, lx1_recv, lx2_send, lx2_recv, lz_send, lz_recv,
):
    dp = lax.axis_index("dp")
    mp = lax.axis_index("mp")
    y, c = dp // 2, dp % 2
    z, x = mp // NX, mp % NX
    other = 1 - c
    half = T // 2
    xr = z * NX + (x + 1) % NX
    xl = z * NX + (x + 3) % NX
    yr = 2 * ((y + 1) % NY) + c
    yl = 2 * ((y + 3) % NY) + c
    active = dp < NT

    def has(q, core):
        return 2 * q + core < NT

    load_h = pltpu.make_async_copy(grad_ref, h.at[:, pl.ds(0, RB)], in_sem.at[0])
    load_h.start()
    load_a = {}
    for j in (2, 3, 4, 1, 5, 0):
        load_a[j] = pltpu.make_async_copy(grad5_ref.at[:, :, (x + j) % NX], a.at[j], in_sem.at[1 + j])
        load_a[j].start()

    barrier = pltpu.get_barrier_semaphore()

    def hello_mp(i, carry):
        pl.semaphore_signal(barrier, inc=1, device_id=(dp, (mp + i) % NMP), device_id_type=pl.DeviceIdType.MESH)
        return carry

    def hello_dp(i, carry):
        pl.semaphore_signal(barrier, inc=1, device_id=((dp + i) % NDP, mp), device_id_type=pl.DeviceIdType.MESH)
        return carry

    lax.fori_loop(1, NDP, hello_dp, 0)
    lax.fori_loop(1, NMP, hello_mp, 0)

    h[:, pl.ds(RB, T)] = jnp.zeros((h.shape[0], T), BF16)
    order = [(y + k) % NY for k in (2, 1, 3, 0)]
    q2, q1, q3, q0 = order

    def right_part(q):
        cols = pl.ds(pl.multiple_of(q * 2 * T, 2 * T), 2 * T)
        block = lax.dot_general(h[:, :RB], h[:, cols], (((0,), (0,)), ((), ())), preferred_element_type=F32)
        for e in range(2):
            pb[e] = block[:, e * T:(e + 1) * T]
            for m in range(NMP):
                part[2 * q + e, m] = pb[e, RPM * m:RPM * (m + 1)]

    def ra_copy(i):
        q = order[i]
        return remote(part.at[2 * q + other], ra.at[q], ra_send.at[i], ra_recv.at[i], dp + 1 - 2 * c, mp)

    def ra_go(i):
        @pl.when(has(order[i], other))
        def _():
            ra_copy(i).start()

    def ra_sum(i):
        q = order[i]

        @pl.when(has(q, c))
        def _():
            ra_copy(i).wait_recv()
            part[2 * q + c] = part[2 * q + c] + ra[q]

    def left_part(j):
        for l in range(3):
            rows = a[j, l].reshape(T, RB)
            cols = a[j:j + 3, l].reshape(3 * T, RB)
            lp[j, l] = lax.dot_general(rows, cols, (((1,), (1,)), ((), ())), preferred_element_type=F32)

    lx1_r = [remote(lp.at[2, l, pl.ds(0, half)], lx1.at[l, 0], lx1_send.at[l, 0], lx1_recv.at[l, 0], dp, xr) for l in range(3)]
    lx1_l = [remote(lp.at[2, l, pl.ds(half, half)], lx1.at[l, 1], lx1_send.at[l, 1], lx1_recv.at[l, 1], dp, xl) for l in range(3)]
    lx2_r = [remote(lp.at[1, l], lx2.at[l, 0], lx2_send.at[l, 0], lx2_recv.at[l, 0], dp, xr) for l in range(3)]
    lx2_l = [remote(lp.at[3, l], lx2.at[l, 1], lx2_send.at[l, 1], lx2_recv.at[l, 1], dp, xl) for l in range(3)]

    chunk = ((0, 16), (16, 12))
    hm = NMP // 2

    def rb1_copy(k, way):
        lo, n = chunk[k]
        src = part.at[2 * q2 + c, pl.ds(way * hm, hm), pl.ds(lo, n)]
        return remote(src, rb1.at[way, :, pl.ds(lo, n)], rb1_send.at[k, way], rb1_recv.at[k, way], (yr, yl)[way], mp)

    def rb2_copy(k, way):
        lo, n = chunk[k]
        src = part.at[2 * (q1, q3)[way] + c, :, pl.ds(lo, n)]
        return remote(src, rb2.at[way, :, pl.ds(lo, n)], rb2_send.at[k, way], rb2_recv.at[k, way], (yr, yl)[way], mp)

    def rb1_go():
        @pl.when(has(q2, c))
        def _():
            for k in range(2):
                for way in range(2):
                    rb1_copy(k, way).start()

    def rb2_go(k):
        lo, n = chunk[k]
        for way in range(2):
            q = (q1, q3)[way]

            @pl.when(has(q, c))
            def _():
                rb1_copy(k, way).wait_recv()
                t = 2 * q + c
                ms = slice(way * hm, (way + 1) * hm)
                part[t, ms, lo:lo + n] = part[t, ms, lo:lo + n] + rb1[way, :, lo:lo + n]
                rb2_copy(k, way).start()

    def lx2_go(l):
        lx1_r[l].wait_recv()
        lp[1, l, :half] = lp[1, l, :half] + lx1[l, 0]
        lx2_r[l].start()
        lx1_l[l].wait_recv()
        lp[3, l, half:] = lp[3, l, half:] + lx1[l, 1]
        lx2_l[l].start()

    def r2_go(k):
        lo, n = chunk[k]
        r2 = (r2a, r2b)[k]

        @pl.when(active)
        def _():
            for way in range(2):
                rb2_copy(k, way).wait_recv()
            part[dp, :, lo:lo + n] = part[dp, :, lo:lo + n] + rb2[0, :, lo:lo + n] + rb2[1, :, lo:lo + n]

            def go(i, carry):
                to = (mp + i) % NMP
                remote(
                    part.at[dp, to, pl.ds(lo, n)], r2.at[NMP - i],
                    r2_send.at[k], r2_recv.at[k], dp, to,
                ).start()
                return carry

            lax.fori_loop(1, NMP, go, 0)
            r2[0] = part[dp, mp, lo:lo + n]

    def r3_copy(k, i):
        o = (dp + i) % NDP
        s3, r3 = ((s3a, r3a), (s3b, r3b))[k]
        return remote(s3.at[o], r3.at[dp], r3_send.at[k, i], r3_recv.at[k, dp], o, mp)

    def r3_go(k):
        lo, n = chunk[k]
        s3, r3 = ((s3a, r3a), (s3b, r3b))[k]
        r2 = (r2a, r2b)[k]

        @pl.when(active)
        def _():
            everything = r2.at[pl.ds(1, NMP - 1)]
            pltpu.make_async_copy(everything, everything, r2_recv.at[k]).wait()
            for o in range(NDP):
                for s in range(CAP):
                    s3[o, n * s:n * (s + 1), :] = r2[tab[0, o * CAP + s]]
            for i in range(1, NDP):
                r3_copy(k, i).start()
            r3[dp] = s3[dp]

    def zz(k):
        return (z + NZ + k) % NZ

    def lz_copy(l, i):
        to, src, dst, dx = {
            0: (1, lz.at[l, zz(3)], rly.at[l, 0], 0),
            1: (-1, lz.at[l, zz(-3)], rly.at[l, 1], 0),
            2: (2, lz.at[l, zz(4), :, pl.ds(0, 2 * T)], rlyh.at[l, 0], 0),
            3: (-2, lz.at[l, zz(4), :, pl.ds(2 * T, 2 * T)], rlyh.at[l, 1], 0),
            4: (1, lz.at[l, zz(1), :, pl.ds(0, 3 * T)], fin.at[l, 0], 0),
            5: (-1, lz.at[l, zz(-1), :, pl.ds(0, 3 * T)], fin.at[l, 1], 0),
            6: (2, lz.at[l, zz(2), :, pl.ds(0, 3 * T)], fin.at[l, 2], 0),
            7: (-2, lz.at[l, zz(-2), :, pl.ds(0, 3 * T)], fin.at[l, 3], 0),
            8: (1, lz.at[l, zz(1), :, pl.ds(3 * T, T)], fint.at[l, 0], 1),
            9: (-1, lz.at[l, zz(-1), :, pl.ds(3 * T, T)], fint.at[l, 1], 1),
            10: (2, lz.at[l, zz(2), :, pl.ds(3 * T, T)], fint.at[l, 2], 1),
            11: (-2, lz.at[l, zz(-2), :, pl.ds(3 * T, T)], fint.at[l, 3], 1),
            12: (0, lz.at[l, z, :, pl.ds(3 * T, T)], fint.at[l, 4], 1),
        }[i]
        return remote(src, dst, lz_send.at[l, i], lz_recv.at[l, i], dp, zz(to) * NX + (x + dx) % NX)

    def lz_first(l):
        lx2_r[l].wait_recv()
        lx2_l[l].wait_recv()
        band = lp[0, l] + lx2[l, 0] + lx2[l, 1]
        lz[l, :, :, :3 * T] = band.reshape(NZ, 16, 3 * T)
        lz[l, :, :, 3 * T:] = band[:, T:2 * T].T.reshape(NZ, 16, T)
        for i in (2, 3, 0, 1, 4, 5, 8, 9, 12):
            lz_copy(l, i).start()

    def lz_second(l):
        for way in range(2):
            t = (zz(2), zz(-2))[way]
            lz_copy(l, way).wait_recv()
            lz_copy(l, 2 + way).wait_recv()
            cs = slice(way * 2 * T, (way + 1) * 2 * T)
            lz[l, t] = lz[l, t] + rly[l, way]
            lz[l, t, :, cs] = lz[l, t, :, cs] + rlyh[l, way]
            lz_copy(l, 6 + way).start()
            lz_copy(l, 10 + way).start()

    def lz_last(l):
        for i in range(4, 13):
            lz_copy(l, i).wait_recv()
        own = lz[l, z, :, :3 * T] + fin[l, 0] + fin[l, 1] + fin[l, 2] + fin[l, 3]
        turned = fint[l, 0] + fint[l, 1] + fint[l, 2] + fint[l, 3] + fint[l, 4]
        row = jnp.concatenate([own, turned], axis=1)
        total = None
        for _ in range(3):
            piece = row.astype(BF16)
            row = row - piece.astype(F32)
            term = jnp.dot(piece, perm[...], preferred_element_type=F32)
            total = term if total is None else total + term
        left_ref[l] = total

    def make_perm():
        p = lax.broadcasted_iota(jnp.int32, (NX * T, NX * T), 0)
        q = lax.broadcasted_iota(jnp.int32, (NX * T, NX * T), 1)
        place = ((p // 16) % NZ) * (16 * NX) + ((p // T + x) % NX) * 16 + p % 16
        perm[...] = (place == q).astype(F32).astype(BF16)

    def make_table():
        lane = lax.broadcasted_iota(jnp.int32, (8, T), 1)
        lane_owner = (lane * 43) >> 8
        lane_rank = lane - lane_owner * CAP
        seen = jnp.zeros((8, T), jnp.int32)
        found = jnp.zeros((8, T), jnp.int32)
        mine = jnp.int32(0)
        for b in range(NMP):
            o = owners_ref[0, b]
            same = lane_owner == o
            found = jnp.where(same & (seen == lane_rank), b, found)
            seen = seen + same.astype(jnp.int32)
            mine = mine + (o == dp).astype(jnp.int32)
        tabv[...] = (found - mp + NMP) % NMP
        cp = pltpu.make_async_copy(tabv, tab, tab_sem)
        cp.start()
        cp.wait()
        return [(k < mine).astype(F32) for k in range(CAP)]

    def right_out(k, valid):
        lo, n = chunk[k]
        r3 = (r3a, r3b)[k]
        for d in range(NT):
            @pl.when(dp != d)
            def _():
                pltpu.make_async_copy(r3.at[d], r3.at[d], r3_recv.at[k, d]).wait()

            for s in range(CAP):
                right_ref[s, lo:lo + n, d * T:(d + 1) * T] = r3[d, n * s:n * (s + 1), :] * valid[s]

    load_h.wait()
    right_part(q2)
    for j in (2, 3, 4):
        load_a[j].wait()
    left_part(2)
    pl.semaphore_wait(barrier, NMP - 1 + NDP - 1)
    ra_go(0)
    for l in range(3):
        lx1_r[l].start()
        lx1_l[l].start()
    right_part(q1)
    ra_go(1)
    right_part(q3)
    ra_go(2)
    ra_sum(0)
    rb1_go()
    right_part(q0)
    ra_go(3)
    for j in (1, 5, 0):
        load_a[j].wait()
    left_part(1)
    left_part(3)
    lx2_go(0)
    ra_sum(1)
    ra_sum(2)
    rb2_go(0)
    lx2_go(1)
    lx2_go(2)
    rb2_go(1)
    left_part(0)
    ra_sum(3)
    valid = make_table()
    make_perm()
    scale_ref[...] = jnp.stack([jnp.full((T,), BETA * v, F32) for v in valid] + [jnp.zeros((T,), F32)] * 2)
    lz_first(0)
    r2_go(0)
    lz_second(0)
    lz_first(1)
    r2_go(1)
    lz_second(1)
    lz_first(2)
    r3_go(0)
    lz_second(2)
    r3_go(1)
    for l in range(3):
        lz_last(l)
    right_out(0, valid)
    right_out(1, valid)

    for i in range(NY):
        @pl.when(has(order[i], other))
        def _():
            ra_copy(i).wait_send()

    @pl.when(has(q2, c))
    def _():
        for k in range(2):
            for way in range(2):
                rb1_copy(k, way).wait_send()

    for way in range(2):
        @pl.when(has((q1, q3)[way], c))
        def _():
            for k in range(2):
                rb2_copy(k, way).wait_send()

    for l in range(3):
        for cp in (lx1_r[l], lx1_l[l], lx2_r[l], lx2_l[l]):
            cp.wait_send()
        for i in range(13):
            lz_copy(l, i).wait_send()

    @pl.when(active)
    def _():
        for k in range(2):
            sent = (r2a, r2b)[k].at[pl.ds(1, NMP - 1)]
            pltpu.make_async_copy(sent, sent, r2_send.at[k]).wait()
            for i in range(1, NDP):
                r3_copy(k, i).wait_send()


def per_device(gradient, owners, left_old, right_old):
    rows = gradient.shape[0]
    dma = pltpu.SemaphoreType.DMA
    left_gram, right_gram, scale = pl.pallas_call(
        kernel,
        out_shape=(
            jax.ShapeDtypeStruct((3, 16, 512), F32),
            jax.ShapeDtypeStruct((CAP, RPM, RB), F32),
            jax.ShapeDtypeStruct((8, T), F32),
        ),
        in_specs=[
            pl.BlockSpec(memory_space=pltpu.HBM),
            pl.BlockSpec(memory_space=pltpu.HBM),
            pl.BlockSpec(memory_space=pltpu.SMEM),
        ],
        out_specs=(pl.BlockSpec(memory_space=pltpu.VMEM),) * 3,
        scratch_shapes=[
            pltpu.VMEM((rows, 1024), BF16),
            pltpu.VMEM((6, 3, NZ, 16, RB), BF16),
            pltpu.VMEM((2, RB, T), F32),
            pltpu.VMEM((8, NMP, RPM, T), F32),
            pltpu.VMEM((NY, NMP, RPM, T), F32),
            pltpu.VMEM((2, NMP // 2, RPM, T), F32),
            pltpu.VMEM((2, NMP, RPM, T), F32),
            pltpu.VMEM((NMP, 16, T), F32),
            pltpu.VMEM((NMP, 12, T), F32),
            pltpu.VMEM((NDP, CAP * 16, T), F32),
            pltpu.VMEM((NDP, CAP * 12, T), F32),
            pltpu.VMEM((NDP, CAP * 16, T), F32),
            pltpu.VMEM((NDP, CAP * 12, T), F32),
            pltpu.VMEM((NX, 3, T, 3 * T), F32),
            pltpu.VMEM((3, 2, T // 2, 3 * T), F32),
            pltpu.VMEM((3, 2, T, 3 * T), F32),
            pltpu.VMEM((3, NZ, 16, 4 * T), F32),
            pltpu.VMEM((3, 2, 16, 4 * T), F32),
            pltpu.VMEM((3, 2, 16, 2 * T), F32),
            pltpu.VMEM((3, 4, 16, 3 * T), F32),
            pltpu.VMEM((3, 5, 16, T), F32),
            pltpu.VMEM((4 * T, 4 * T), BF16),
            pltpu.VMEM((8, T), jnp.int32),
            pltpu.SMEM((8, T), jnp.int32),
            dma((7,)), dma,
            dma((NY,)), dma((NY,)),
            dma((2, 2)), dma((2, 2)), dma((2, 2)), dma((2, 2)),
            dma((2,)), dma((2,)), dma((2, NDP)), dma((2, NDP)),
            dma((3, 2)), dma((3, 2)), dma((3, 2)), dma((3, 2)),
            dma((3, 13)), dma((3, 13)),
        ],
        compiler_params=pltpu.CompilerParams(
            collective_id=0, has_side_effects=True, vmem_limit_bytes=56 * 1024 * 1024
        ),
        name="stats",
    )(gradient, gradient.reshape(3, NZ, NX, 16, RB), owners.reshape(1, NMP))
    left_stats = BETA * left_old + left_gram
    right_stats = scale[:CAP, :1, None] * right_old + right_gram
    return left_stats, right_stats


def solution(mesh):
    in_specs = (P("dp", "mp"), P(), P("dp", "mp", None), P("dp", "mp", None))
    out_specs = (P("dp", "mp", None), P("dp", "mp", None))
    return jax.shard_map(
        per_device, mesh=mesh, in_specs=in_specs, out_specs=out_specs, check_vma=False
    )
```

time: 357 us -> 61 us (0.17)
  waiting for transfers between devices: 281 us -> 0 us
  Pallas kernels: 0 us -> 55.7 us
  local copies, waits for them, and re-layouts: 21.3 us -> 0.8 us
  between operations: 16.2 us -> 0.66 us
  matrix products: 13.4 us -> 0 us
  starting transfers between devices: 9.91 us -> 0 us
  other arithmetic: 12.6 us -> 3.63 us
    unnamed x3 -> x0, waiting for transfers between devices: 204 us -> none
    psum x1 -> x0, waiting for transfers between devices: 76.5 us -> none  [per_device(): summed_blocks = lax.psum(partial_gram, 'dp')]
    pallas_call x0 -> x1, Pallas kernels: none -> 55.7 us  [per_device(): pl.pallas_call(kernel, out_shape=(jax.ShapeDtypeStruct((3, 16, 512), F32)...]
    dot_general x3 -> x0, matrix products: 13.4 us -> none  [the longest x1 5.11 us: per_device(): jnp.einsum('kb,bad->kad', select_mine, pieces, precision=lax.Precision.HI...]
    all_to_all x1 -> x0, other arithmetic: 11.2 us -> none  [per_device(): lax.all_to_all(summed_blocks, 'mp', split_axis=1, concat_axis=0, tiled=True)]
    all_to_all x1 -> x0, starting transfers between devices: 9.65 us -> none  [per_device(): lax.all_to_all(summed_blocks, 'mp', split_axis=1, concat_axis=0, tiled=True)]
    psum x1 -> x0, local copies, waits for them, and re-layouts: 6.95 us -> none  [per_device(): summed_blocks = lax.psum(partial_gram, 'dp')]
    transpose x1 -> x0, local copies, waits for them, and re-layouts: 5.1 us -> none  [per_device(): jnp.einsum('lrc,lsc->rls', grad_blocks, grad_blocks, preferred_element_ty...]
  transfers between devices with their start and end apart: 3 -> 0, of which waited for: 2 -> 0; matrix products, arithmetic and copies ran while one was open for 3% -> 0% of each run, Pallas kernels for 0% -> 0%
where the time goes in v2:
time: 61 us; the launch traced here: 60.8 us
  Pallas kernels  55.7 us (91%)
  other arithmetic  3.63 us (6%)
  local copies, waits for them, and re-layouts  0.8 us (1%)
  between operations  0.66 us (1%)
    pallas_call x1, Pallas kernels, per_device(): pl.pallas_call(kernel, out_shape=(jax.ShapeDtypeStruct((3, 16, 512), F32)...  55.7 us
    add x1, other arithmetic, per_device(): right_stats = scale[:CAP, :1, None] * right_old + right_gram  2.08 us
    add x1, other arithmetic, per_device(): left_stats = BETA * left_old + left_gram  1.55 us

profile of v2, /device:TPU:1, one launch (start us, length us, event | category | flops | bytes accessed | tf_op | source)
XLA Modules:
  0.0 60.8 jit_solution(12775969017819292486)
XLA Ops:
  0.6 0.0 copy-start.1
  0.6 0.0 copy-start
  0.7 55.7 %stats.1 = (f32[3,16,512]{2,1,0:T(8,128)}, f32[6,28,896]{2,1,0:T(8,128)}, f32[8,128]{1,0:T(8,128)}) custom-call(bf16[1536,896]{1,0:T(8,128)(2,1)} %grad_ref.1, bf16[3,8,4,16,896]{4,3,2,1,0:T(8,128)(2,1)} %bitcast.2, s32[1,32]{1,0:T(1,128)} %bitcast.3), custom_call_target="tpu_custom_call" | custom-call | tf_op jit(solution)/shard_map/stats/pallas_call | solution.py:377
  56.3 0.0 copy-done.1
  56.3 1.5 %multiply_add_fusion.1 = f32[3,16,512]{2,1,0:T(8,128)} fusion(f32[3,16,512]{2,1,0:T(8,128)} %get-tuple-element.5, f32[3,16,512]{2,1,0:T(8,128)S(1)} %copy-done.1), kind=kLoop, calls=%fused_computation.1 | loop fusion | flops 49152 | bytes 294912 | tf_op jit(solution)/shard_map/add | solution.py:427
  57.9 0.8 %slice_reduce_fusion = f32[6]{0:T(128)S(1)} fusion(f32[8,128]{1,0:T(8,128)} %get-tuple-element.6), kind=kLoop, calls=%fused_computation.2 | loop fusion | bytes 48 | tf_op jit(solution)/shard_map/slice | solution.py:428
  58.7 0.0 copy-done
  58.7 2.1 %multiply_add_fusion = f32[6,28,896]{2,1,0:T(8,128)} fusion(f32[6,28,896]{2,1,0:T(8,128)} %get-tuple-element.7, f32[6,28,896]{2,1,0:T(8,128)S(1)} %copy-done, f32[6]{0:T(128)S(1)} %slice_reduce_fusion), kind=kLoop, calls=%fused_computation | loop fusion | flops 301056 | bytes 1806360 | tf_op jit(solution)/shard_map/add | solution.py:428
Async XLA Ops:
  0.6 55.7 %copy-start.1 = (f32[3,16,512]{2,1,0:T(8,128)S(1)}, f32[3,16,512]{2,1,0:T(8,128)}, u32[]{:S(2)}) copy-start(f32[3,16,512]{2,1,0:T(8,128)} %param.6) | copy-start | bytes 294916
  0.6 58.0 %copy-start = (f32[6,28,896]{2,1,0:T(8,128)S(1)}, f32[6,28,896]{2,1,0:T(8,128)}, u32[]{:S(2)}) copy-start(f32[6,28,896]{2,1,0:T(8,128)} %param.7) | copy-start | bytes 1806340

commit v3 on v2

v3 whole, which is shorter than its diff:
```python
import jax
import jax.numpy as jnp
from jax import lax
from jax.experimental import pallas as pl
from jax.experimental.pallas import tpu as pltpu
from jax.sharding import PartitionSpec as P

BETA = 0.95
F32 = jnp.float32
BF16 = jnp.bfloat16
RB = 896
T = 128
NT = 7
NMP = 32
NDP = 8
CAP = 6
RPM = 28
NY = 4
NX = 4
NZ = 8

CHUNK = ((0, 16), (16, 12))

LEFT_TILES = (
    ((0, 0), (2, 2), (1, 3)),
    ((0, 1), (2, 3)),
    ((1, 1), (3, 3), (2, 0)),
    ((0, 3), (2, 1)),
)


def remote(src, dst, send_sem, recv_sem, dp, mp):
    return pltpu.make_async_remote_copy(
        src_ref=src,
        dst_ref=dst,
        send_sem=send_sem,
        recv_sem=recv_sem,
        device_id=(dp, mp),
        device_id_type=pl.DeviceIdType.MESH,
    )


def kernel(
    grad_ref, grad5_ref, owners_ref, left_ref, right_ref, scale_ref,
    h, a, part, ra, rb1, rb2, tall, t28, r2a, r2b, s3a, s3b, r3a, r3b,
    lp, lx1, lx2, lz, rly, rlyh, fin, perm, tabv, tab,
    in_sem, tab_sem, ra_send, ra_recv, rb_send, rb_recv,
    r2_send, r2_recv, r3_send, r3_recv,
    lx_send, lx_recv, lz_send, lz_recv, fin_send, fin_recv,
):
    dp = lax.axis_index("dp")
    mp = lax.axis_index("mp")
    y, c = dp // 2, dp % 2
    z, x = mp // NX, mp % NX
    other = 1 - c
    half = T // 2
    xs = (z * NX + (x + 1) % NX, z * NX + (x + 3) % NX)
    ys = (2 * ((y + 1) % NY) + c, 2 * ((y + 3) % NY) + c)
    active = dp < NT

    def has(q, core):
        return 2 * q + core < NT

    rows = h.shape[0]
    load_h = []
    for i in range(4):
        n = rows // 4
        cp = pltpu.make_async_copy(grad_ref.at[pl.ds(i * n, n)], h.at[pl.ds(i * n, n)], in_sem.at[i])
        cp.start()
        load_h.append(cp)
    load_a = []
    for g in range(NX):
        cp = pltpu.make_async_copy(grad5_ref.at[:, :, g], a.at[:, g], in_sem.at[4 + g])
        cp.start()
        load_a.append(cp)

    barrier = pltpu.get_barrier_semaphore()

    def hello_mp(i, carry):
        pl.semaphore_signal(barrier, inc=1, device_id=(dp, (mp + i) % NMP), device_id_type=pl.DeviceIdType.MESH)
        return carry

    def hello_dp(i, carry):
        pl.semaphore_signal(barrier, inc=1, device_id=((dp + i) % NDP, mp), device_id_type=pl.DeviceIdType.MESH)
        return carry

    lax.fori_loop(1, NDP, hello_dp, 0)
    lax.fori_loop(1, NMP, hello_mp, 0)

    def right_part(q):
        lo = 2 * T * q
        wide = min(2 * T, RB - lo)
        block = lax.dot_general(
            h[:, lo:RB], h[:, lo:lo + wide], (((0,), (0,)), ((), ())), preferred_element_type=F32
        )
        for col in range(2 * q, 2 * q + wide // T):
            for row in range(col, NT):
                d = (row + col) % NT
                u = (4 * d) % NT
                k = min((row - u) % NT, (u - row) % NT)
                i, j = (row - 2 * q) * T, (col - 2 * q) * T
                part[d, k] = block[i:i + T, j:j + T]

    order = [(y + k) % NY for k in (2, 1, 3, 0)]
    q2, q1, q3, q0 = order

    def ra_copy(i):
        q = order[i]
        return remote(part.at[2 * q + other], ra.at[q], ra_send.at[i], ra_recv.at[i], dp + 1 - 2 * c, mp)

    def ra_go(i):
        @pl.when(has(order[i], other))
        def _():
            ra_copy(i).start()

    def rb_copy(step, way):
        i = 2 * step + way
        tiles = pl.ds(2 * way, 2) if step != 1 else pl.ds(2 - 2 * way, 2)
        q = (q2, (q1, q3)[way], (q1, q3)[way])[step]
        dst = rb1.at[way] if step == 0 else rb2.at[way, tiles]
        return remote(part.at[2 * q + c, tiles], dst, rb_send.at[i], rb_recv.at[i], ys[way], mp)

    def ra_sum(i):
        q = order[i]

        @pl.when(has(q, c))
        def _():
            ra_copy(i).wait_recv()
            part[2 * q + c] = part[2 * q + c] + ra[q]
            if i == 0:
                rb_copy(0, 0).start()
                rb_copy(0, 1).start()
            elif i < 3:
                rb_copy(1, i - 1).start()

    def rb_second():
        for way in range(2):
            q = (q1, q3)[way]

            @pl.when(has(q, c))
            def _():
                rb_copy(0, way).wait_recv()
                t = 2 * q + c
                part[t, 2 * way:2 * way + 2] = part[t, 2 * way:2 * way + 2] + rb1[way]
                rb_copy(2, way).start()

    def right_whole():
        @pl.when(active)
        def _():
            for way in range(2):
                rb_copy(1, way).wait_recv()
                rb_copy(2, way).wait_recv()
            u = (4 * dp) % NT
            for k in range(4):
                tile = part[dp, k] + rb2[0, k] + rb2[1, k]
                one = (u + k) % NT
                two = (u + NT - k) % NT
                if k == 0:
                    tall[pl.ds(pl.multiple_of(one * T, T), T), :] = tile
                else:
                    big = jnp.maximum(one, two)
                    small = jnp.minimum(one, two)
                    tall[pl.ds(pl.multiple_of(big * T, T), T), :] = tile
                    tall[pl.ds(pl.multiple_of(small * T, T), T), :] = tile.T
            for m in range(NMP):
                t28[m] = tall[RPM * m:RPM * (m + 1)]

    def r2_go(k):
        lo, n = CHUNK[k]
        r2 = (r2a, r2b)[k]

        @pl.when(active)
        def _():
            def go(i, carry):
                to = (mp + i) % NMP
                remote(t28.at[to, pl.ds(lo, n)], r2.at[NMP - i], r2_send.at[k], r2_recv.at[k], dp, to).start()
                return carry

            lax.fori_loop(1, NMP, go, 0)
            r2[0] = t28[mp, lo:lo + n]

    def r3_copy(k, i):
        o = (dp + i) % NDP
        s3, r3 = ((s3a, r3a), (s3b, r3b))[k]
        return remote(s3.at[o], r3.at[dp], r3_send.at[k, i], r3_recv.at[k, dp], o, mp)

    def r3_go(k):
        n = CHUNK[k][1]
        s3, r3 = ((s3a, r3a), (s3b, r3b))[k]
        r2 = (r2a, r2b)[k]

        @pl.when(active)
        def _():
            everything = r2.at[pl.ds(1, NMP - 1)]
            pltpu.make_async_copy(everything, everything, r2_recv.at[k]).wait()
            for o in range(NDP):
                for s in range(CAP):
                    s3[o, n * s:n * (s + 1), :] = r2[tab[0, o * CAP + s]]
            for i in range(1, NDP):
                r3_copy(k, i).start()
            r3[dp] = s3[dp]

    def left_part(l):
        g = a[l].reshape(NX * T, RB)
        block = lax.dot_general(g, g, (((1,), (1,)), ((), ())), preferred_element_type=F32)
        for v in range(4):
            for i, (r, s) in enumerate(LEFT_TILES[v]):
                lp[l, v, i] = block[r * T:(r + 1) * T, s * T:(s + 1) * T]

    def by_parity(value, fn):
        @pl.when(value % 2 == 0)
        def _():
            fn(3)

        @pl.when(value % 2 == 1)
        def _():
            fn(2)

    def lx_copy(l, step, way, n):
        i = 2 * step + way
        v = ((x + 2, x + 1, x + 1), (x + 2, x + 3, x + 3))[way][step]
        v = (v + 4 - l) % 4
        lo = half * way if step != 1 else half * (1 - way)
        tiles = pl.ds(0, n)
        part_rows = pl.ds(lo, half)
        dst = lx1.at[l, way, tiles] if step == 0 else lx2.at[l, way, tiles, part_rows]
        src = lp.at[l, v, tiles, part_rows]
        return remote(src, dst, lx_send.at[l, i], lx_recv.at[l, i], dp, xs[way])

    def lx_start(l, step):
        def go(n):
            lx_copy(l, step, 0, n).start()
            lx_copy(l, step, 1, n).start()

        by_parity(x + 4 - l + (0 if step == 0 else 1), go)

    def lx_second(l):
        def go(n):
            for way in range(2):
                lx_copy(l, 0, way, n).wait_recv()
                v = (x + (1, 3)[way] + 4 - l) % 4
                cut = slice(half * way, half * (way + 1))
                lp[l, v, :n, cut] = lp[l, v, :n, cut] + lx1[l, way, :n]
                lx_copy(l, 2, way, n).start()

        by_parity(x + 1 + 4 - l, go)

    def zz(k):
        return (z + NZ + k) % NZ

    def lz_copy(l, i):
        to, src, dst = (
            (1, lz.at[l, zz(3)], rly.at[l, 0]),
            (-1, lz.at[l, zz(-3)], rly.at[l, 1]),
            (2, lz.at[l, zz(4), pl.ds(0, 2)], rlyh.at[l, 0]),
            (-2, lz.at[l, zz(4), pl.ds(2, 2)], rlyh.at[l, 1]),
        )[i]
        return remote(src, dst, lz_send.at[l, i], lz_recv.at[l, i], dp, zz(to) * NX + x)

    hops = (0, 1, -1, 2, -2)

    def fin_start(l, j):
        for r in range(0 if j else 1, 4):
            g = (x + 4 - r) % 4
            to = zz(hops[j])
            remote(lz.at[l, to, g], fin.at[l, 4 * j + r], fin_send.at[l], fin_recv.at[l], dp, to * NX + g).start()

    def lz_first(l):
        def go(n):
            for way in range(2):
                lx_copy(l, 1, way, n).wait_recv()
                lx_copy(l, 2, way, n).wait_recv()
            v = (x + 4 - l) % 4
            tiles = [lp[l, v, i] + lx2[l, 0, i] + lx2[l, 1, i] for i in range(n)]

            def put(g, tile):
                lz[l, :, g] = tile.reshape(NZ, 16, T)

            if n == 3:
                w = v // 2
                put(w, tiles[0])
                put(w + 2, tiles[1])
                put(w + 1, tiles[2])
                put((w + 3) % 4, tiles[2].T)
            else:
                put(0, tiles[0])
                put(v, tiles[0].T)
                put(2, tiles[1])
                put((v + 2) % 4, tiles[1].T)

        by_parity(x + 4 - l, go)
        for i in (2, 3, 0, 1):
            lz_copy(l, i).start()
        for j in (1, 2, 0):
            fin_start(l, j)
        fin[l, 0] = lz[l, z, x]

    def lz_second(l):
        for way in range(2):
            t = (zz(2), zz(-2))[way]
            lz_copy(l, way).wait_recv()
            lz_copy(l, 2 + way).wait_recv()
            lz[l, t] = lz[l, t] + rly[l, way]
            lz[l, t, 2 * way:2 * way + 2] = lz[l, t, 2 * way:2 * way + 2] + rlyh[l, way]
            fin_start(l, 3 + way)

    def lz_last(l):
        everything = fin.at[l, pl.ds(1, 19)]
        pltpu.make_async_copy(everything, everything, fin_recv.at[l]).wait()
        row = []
        for g in range(4):
            r = (g + l) % 4
            row.append(fin[l, r] + fin[l, 4 + r] + fin[l, 8 + r] + fin[l, 12 + r] + fin[l, 16 + r])
        row = jnp.concatenate(row, axis=1)
        total = None
        for _ in range(3):
            piece = row.astype(BF16)
            row = row - piece.astype(F32)
            term = jnp.dot(piece, perm[...], preferred_element_type=F32)
            total = term if total is None else total + term
        left_ref[l] = total

    def make_perm():
        p = lax.broadcasted_iota(jnp.int32, (NX * T, NX * T), 0)
        q = lax.broadcasted_iota(jnp.int32, (NX * T, NX * T), 1)
        place = ((p // 16) % NZ) * (16 * NX) + (p // T) * 16 + p % 16
        perm[...] = (place == q).astype(F32).astype(BF16)

    def make_table():
        lane = lax.broadcasted_iota(jnp.int32, (8, T), 1)
        lane_owner = (lane * 43) >> 8
        lane_rank = lane - lane_owner * CAP
        seen = jnp.zeros((8, T), jnp.int32)
        found = jnp.zeros((8, T), jnp.int32)
        mine = jnp.int32(0)
        for b in range(NMP):
            o = owners_ref[0, b]
            same = lane_owner == o
            found = jnp.where(same & (seen == lane_rank), b, found)
            seen = seen + same.astype(jnp.int32)
            mine = mine + (o == dp).astype(jnp.int32)
        tabv[...] = (found - mp + NMP) % NMP
        cp = pltpu.make_async_copy(tabv, tab, tab_sem)
        cp.start()
        cp.wait()
        valid = [(k < mine).astype(F32) for k in range(CAP)]
        for k in range(CAP):
            scale_ref[k] = BETA * valid[k]
        return valid

    def right_out(k, valid):
        lo, n = CHUNK[k]
        r3 = (r3a, r3b)[k]
        for d in range(NT):
            @pl.when(dp != d)
            def _():
                pltpu.make_async_copy(r3.at[d], r3.at[d], r3_recv.at[k, d]).wait()

        first = (RPM * mp + lo) // T
        last = (RPM * mp + lo + n - 1) // T
        row = lax.broadcasted_iota(jnp.int32, (n, T), 0) + (RPM * mp + lo)
        upper = row < last * T
        for g in range(NT):
            one = (g + first) % NT
            two = (g + last) % NT
            for s in range(CAP):
                cut = slice(n * s, n * (s + 1))
                value = jnp.where(upper, r3[one, cut, :], r3[two, cut, :])
                right_ref[s, lo:lo + n, g * T:(g + 1) * T] = value * valid[s]

    for cp in load_h:
        cp.wait()
    for q in range(4):
        right_part(q)
    pl.semaphore_wait(barrier, NMP - 1 + NDP - 1)
    for i in range(4):
        ra_go(i)
    for cp in load_a:
        cp.wait()
    left_part(0)
    lx_start(0, 0)
    lx_start(0, 1)
    left_part(1)
    lx_start(1, 0)
    left_part(2)
    lx_start(2, 0)
    for i in range(4):
        ra_sum(i)
    valid = make_table()
    lx_second(0)
    lx_start(1, 1)
    rb_second()
    lx_second(1)
    lx_start(2, 1)
    lx_second(2)
    make_perm()
    lz_first(0)
    right_whole()
    r2_go(0)
    r2_go(1)
    lz_first(1)
    lz_second(0)
    lz_second(1)
    r3_go(0)
    lz_first(2)
    r3_go(1)
    lz_second(2)
    for l in range(3):
        lz_last(l)
    right_out(0, valid)
    right_out(1, valid)

    for i in range(NY):
        @pl.when(has(order[i], other))
        def _():
            ra_copy(i).wait_send()

    @pl.when(has(q2, c))
    def _():
        rb_copy(0, 0).wait_send()
        rb_copy(0, 1).wait_send()

    for way in range(2):
        @pl.when(has((q1, q3)[way], c))
        def _():
            rb_copy(1, way).wait_send()
            rb_copy(2, way).wait_send()

    for l in range(3):
        for step in range(3):
            def done(n):
                lx_copy(l, step, 0, n).wait_send()
                lx_copy(l, step, 1, n).wait_send()

            by_parity(x + 4 - l + (0 if step == 0 else 1), done)
        for i in range(4):
            lz_copy(l, i).wait_send()
        sent = fin.at[l, pl.ds(1, 19)]
        pltpu.make_async_copy(sent, sent, fin_send.at[l]).wait()

    @pl.when(active)
    def _():
        for k in range(2):
            sent = (r2a, r2b)[k].at[pl.ds(1, NMP - 1)]
            pltpu.make_async_copy(sent, sent, r2_send.at[k]).wait()
            for i in range(1, NDP):
                r3_copy(k, i).wait_send()


def per_device(gradient, owners, left_old, right_old):
    rows = gradient.shape[0]
    dma = pltpu.SemaphoreType.DMA
    na, nb = CHUNK[0][1], CHUNK[1][1]
    left_gram, right_gram, scale = pl.pallas_call(
        kernel,
        out_shape=(
            jax.ShapeDtypeStruct((3, 16, 512), F32),
            jax.ShapeDtypeStruct((CAP, RPM, RB), F32),
            jax.ShapeDtypeStruct((CAP,), F32),
        ),
        in_specs=[
            pl.BlockSpec(memory_space=pl.ANY),
            pl.BlockSpec(memory_space=pl.ANY),
            pl.BlockSpec(memory_space=pltpu.SMEM),
        ],
        out_specs=(
            pl.BlockSpec(memory_space=pltpu.VMEM),
            pl.BlockSpec(memory_space=pltpu.VMEM),
            pl.BlockSpec(memory_space=pltpu.SMEM),
        ),
        scratch_shapes=[
            pltpu.VMEM((rows, RB), BF16),
            pltpu.VMEM((3, NX, NZ, 16, RB), BF16),
            pltpu.VMEM((NDP, 4, T, T), F32),
            pltpu.VMEM((NY, 4, T, T), F32),
            pltpu.VMEM((2, 2, T, T), F32),
            pltpu.VMEM((2, 4, T, T), F32),
            pltpu.VMEM((RB, T), F32),
            pltpu.VMEM((NMP, RPM, T), F32),
            pltpu.VMEM((NMP, na, T), F32),
            pltpu.VMEM((NMP, nb, T), F32),
            pltpu.VMEM((NDP, CAP * na, T), F32),
            pltpu.VMEM((NDP, CAP * nb, T), F32),
            pltpu.VMEM((NDP, CAP * na, T), F32),
            pltpu.VMEM((NDP, CAP * nb, T), F32),
            pltpu.VMEM((3, 4, 3, T, T), F32),
            pltpu.VMEM((3, 2, 3, T // 2, T), F32),
            pltpu.VMEM((3, 2, 3, T, T), F32),
            pltpu.VMEM((3, NZ, 4, 16, T), F32),
            pltpu.VMEM((3, 2, 4, 16, T), F32),
            pltpu.VMEM((3, 2, 2, 16, T), F32),
            pltpu.VMEM((3, 20, 16, T), F32),
            pltpu.VMEM((4 * T, 4 * T), BF16),
            pltpu.VMEM((8, T), jnp.int32),
            pltpu.SMEM((8, T), jnp.int32),
            dma((8,)), dma,
            dma((NY,)), dma((NY,)), dma((6,)), dma((6,)),
            dma((2,)), dma((2,)), dma((2, NDP)), dma((2, NDP)),
            dma((3, 6)), dma((3, 6)), dma((3, 4)), dma((3, 4)), dma((3,)), dma((3,)),
        ],
        compiler_params=pltpu.CompilerParams(
            collective_id=0, has_side_effects=True, vmem_limit_bytes=105 * 512 * 1024
        ),
        name="stats",
    )(gradient, gradient.reshape(3, NZ, NX, 16, RB), owners.reshape(1, NMP))
    left_stats = BETA * left_old + left_gram
    right_stats = scale[:, None, None] * right_old + right_gram
    return left_stats, right_stats


def solution(mesh):
    in_specs = (P("dp", "mp"), P(), P("dp", "mp", None), P("dp", "mp", None))
    out_specs = (P("dp", "mp", None), P("dp", "mp", None))
    return jax.shard_map(
        per_device, mesh=mesh, in_specs=in_specs, out_specs=out_specs, check_vma=False
    )
```

time: 61 us -> 54 us (0.89)
  Pallas kernels: 55.7 us -> 50.8 us
  other arithmetic: 3.63 us -> 1.67 us
    pallas_call x1, Pallas kernels: 55.7 us -> 50.8 us  [per_device(): pl.pallas_call(kernel, out_shape=(jax.ShapeDtypeStruct((3, 16, 512), F32)...]
    add x1, other arithmetic: 2.08 us -> 1.01 us  [per_device(): right_stats = scale[:, None, None] * right_old + right_gram]
    add x1, other arithmetic: 1.55 us -> 0.66 us  [per_device(): left_stats = BETA * left_old + left_gram]
    slice x1 -> x0, local copies, waits for them, and re-layouts: 0.79 us -> none  [per_device(): right_stats = scale[:CAP, :1, None] * right_old + right_gram]
    unnamed x4 -> x6, local copies, waits for them, and re-layouts: 0.01 us -> 0.66 us
where the time goes in v3:
time: 54 us; the launch traced here: 53.8 us
  Pallas kernels  50.8 us (94%)
  other arithmetic  1.67 us (3%)
  local copies, waits for them, and re-layouts  0.66 us (1%)
  between operations  0.66 us (1%)
    pallas_call x1, Pallas kernels, per_device(): pl.pallas_call(kernel, out_shape=(jax.ShapeDtypeStruct((3, 16, 512), F32)...  50.8 us

profile of v3, /device:TPU:1, one launch (start us, length us, event | category | flops | bytes accessed | tf_op | source)
XLA Modules:
  0.0 53.8 jit_solution(4249006258452145904)
XLA Ops:
  0.6 0.0 copy-start
  0.6 0.6 %copy-done = s32[32,1]{0,1:T(1,128)S(1)} copy-done((s32[32,1]{0,1:T(1,128)S(1)}, s32[32,1]{0,1:T(1,128)}, u32[]{:S(2)}) %copy-start) | copy-done | bytes 152
  1.3 0.0 copy-start.2
  1.3 0.0 copy-start.1
  1.3 50.8 %stats.1 = (f32[3,16,512]{2,1,0:T(8,128)S(1)}, f32[6,28,896]{2,1,0:T(8,128)S(1)}, f32[6]{0:T(128)S(1)}) custom-call(bf16[1536,896]{1,0:T(8,128)(2,1)} %grad_ref.1, bf16[3,8,4,16,896]{4,3,2,1,0:T(8,128)(2,1)} %bitcast.3, s32[1,32]{1,0:T(1,128)S(1)} %bitcast.2), custom_call_target="tpu_custom_call" | custom-call | tf_op jit(solution)/shard_map/stats/pallas_call | solution.py:454
  52.1 0.0 copy-done.2
  52.1 0.7 %multiply_add_fusion.1 = f32[3,16,512]{2,1,0:T(8,128)} fusion(f32[3,16,512]{2,1,0:T(8,128)S(1)} %get-tuple-element.5, f32[3,16,512]{2,1,0:T(8,128)S(1)} %copy-done.2), kind=kLoop, calls=%fused_computation.1 | loop fusion | flops 49152 | bytes 294912 | tf_op jit(solution)/shard_map/add | solution.py:506
  52.8 0.0 copy-done.1
  52.8 1.0 %multiply_add_fusion = f32[6,28,896]{2,1,0:T(8,128)} fusion(f32[6,28,896]{2,1,0:T(8,128)S(1)} %get-tuple-element.7, f32[6,28,896]{2,1,0:T(8,128)S(1)} %copy-done.1, f32[6]{0:T(128)S(1)} %get-tuple-element.6), kind=kLoop, calls=%fused_computation | loop fusion | flops 301056 | bytes 1806360 | tf_op jit(solution)/shard_map/add | solution.py:507
Async XLA Ops:
  0.6 0.7 %copy-start = (s32[32,1]{0,1:T(1,128)S(1)}, s32[32,1]{0,1:T(1,128)}, u32[]{:S(2)}) copy-start(s32[32,1]{0,1:T(1,128)} %param.5) | copy-start | bytes 388
  1.3 50.9 %copy-start.2 = (f32[3,16,512]{2,1,0:T(8,128)S(1)}, f32[3,16,512]{2,1,0:T(8,128)}, u32[]{:S(2)}) copy-start(f32[3,16,512]{2,1,0:T(8,128)} %param.6) | copy-start | bytes 294916
  1.3 51.5 %copy-start.1 = (f32[6,28,896]{2,1,0:T(8,128)S(1)}, f32[6,28,896]{2,1,0:T(8,128)}, u32[]{:S(2)}) copy-start(f32[6,28,896]{2,1,0:T(8,128)} %param.7) | copy-start | bytes 1806340

commit v4 on v3

--- a/solution.py
+++ b/solution.py
@@ -41,12 +41,13 @@
 
 
 def kernel(
-    grad_ref, grad5_ref, owners_ref, left_ref, right_ref, scale_ref,
+    grad_ref, owners_ref, left_ref, right_ref, scale_ref,
     h, a, part, ra, rb1, rb2, tall, t28, r2a, r2b, s3a, s3b, r3a, r3b,
-    lp, lx1, lx2, lz, rly, rlyh, fin, perm, tabv, tab,
+    lp, lx1, lx2, lz, rly, rlyh, fin, zg, zr1, zr2, zx, perm, tabv, tab,
     in_sem, tab_sem, ra_send, ra_recv, rb_send, rb_recv,
     r2_send, r2_recv, r3_send, r3_recv,
     lx_send, lx_recv, lz_send, lz_recv, fin_send, fin_recv,
+    zr_send, zr_recv, zx_send, zx_recv,
 ):
     dp = lax.axis_index("dp")
     mp = lax.axis_index("mp")
@@ -68,11 +69,6 @@
         cp = pltpu.make_async_copy(grad_ref.at[pl.ds(i * n, n)], h.at[pl.ds(i * n, n)], in_sem.at[i])
         cp.start()
         load_h.append(cp)
-    load_a = []
-    for g in range(NX):
-        cp = pltpu.make_async_copy(grad5_ref.at[:, :, g], a.at[:, g], in_sem.at[4 + g])
-        cp.start()
-        load_a.append(cp)
 
     barrier = pltpu.get_barrier_semaphore()
 
@@ -201,6 +197,10 @@
             r3[dp] = s3[dp]
 
     def left_part(l):
+        for g in range(NX):
+            for i in range(NZ):
+                lo = NX * T * l + 16 * NX * i + 16 * g
+                a[l, g, i] = h[lo:lo + 16, :]
         g = a[l].reshape(NX * T, RB)
         block = lax.dot_general(g, g, (((1,), (1,)), ((), ())), preferred_element_type=F32)
         for v in range(4):
@@ -319,6 +319,51 @@
             term = jnp.dot(piece, perm[...], preferred_element_type=F32)
             total = term if total is None else total + term
         left_ref[l] = total
+
+    zh = 8 * NX
+
+    def z_part():
+        g = h[2 * NX * T:3 * NX * T, :]
+        block = lax.dot_general(g, g, (((1,), (1,)), ((), ())), preferred_element_type=F32)
+        zg[...] = block.reshape(NZ, 16 * NX, NX * T)
+
+    def zr_copy(s, way):
+        sign = 1 - 2 * way
+        src = zg.at[zz(sign * (5 - s))]
+        if s == 1:
+            src, dst = zg.at[zz(4), pl.ds(way * zh, zh)], zr1.at[way]
+        else:
+            dst = zr2.at[way, s - 2]
+        return remote(src, dst, zr_send.at[way, s - 1], zr_recv.at[way, s - 1], dp, zz(sign) * NX + x)
+
+    def zr_start(s):
+        for way in range(2):
+            zr_copy(s, way).start()
+
+    def zr_next(s):
+        for way in range(2):
+            sign = 1 - 2 * way
+            t = zz(sign * (4 - s))
+            zr_copy(s, way).wait_recv()
+            if s == 1:
+                cut = slice(way * zh, (way + 1) * zh)
+                zg[t, cut] = zg[t, cut] + zr1[way]
+            else:
+                zg[t] = zg[t] + zr2[way, s - 2]
+            if s < 4:
+                zr_copy(s + 1, way).start()
+
+    def x_rows(to):
+        return pl.ds(pl.multiple_of(16 * to, 16), 16)
+
+    def zx_start():
+        for r in range(1, NX):
+            to = (x + r) % NX
+            remote(zg.at[z, x_rows(to)], zx.at[r - 1], zx_send, zx_recv, dp, z * NX + to).start()
+
+    def zx_last():
+        pltpu.make_async_copy(zx, zx, zx_recv).wait()
+        left_ref[2] = zg[z, x_rows(x)] + zx[0] + zx[1] + zx[2]
 
     def make_perm():
         p = lax.broadcasted_iota(jnp.int32, (NX * T, NX * T), 0)
@@ -375,38 +420,40 @@
     pl.semaphore_wait(barrier, NMP - 1 + NDP - 1)
     for i in range(4):
         ra_go(i)
-    for cp in load_a:
-        cp.wait()
+    z_part()
+    zr_start(1)
     left_part(0)
     lx_start(0, 0)
     lx_start(0, 1)
+    ra_sum(0)
+    ra_sum(1)
+    ra_sum(2)
     left_part(1)
     lx_start(1, 0)
-    left_part(2)
-    lx_start(2, 0)
-    for i in range(4):
-        ra_sum(i)
+    lx_start(1, 1)
+    ra_sum(3)
     valid = make_table()
+    zr_next(1)
     lx_second(0)
-    lx_start(1, 1)
     rb_second()
     lx_second(1)
-    lx_start(2, 1)
-    lx_second(2)
     make_perm()
+    zr_next(2)
     lz_first(0)
     right_whole()
     r2_go(0)
     r2_go(1)
+    zr_next(3)
+    lz_second(0)
     lz_first(1)
-    lz_second(0)
+    zr_next(4)
+    zx_start()
     lz_second(1)
     r3_go(0)
-    lz_first(2)
+    lz_last(0)
+    lz_last(1)
+    zx_last()
     r3_go(1)
-    lz_second(2)
-    for l in range(3):
-        lz_last(l)
     right_out(0, valid)
     right_out(1, valid)
 
@@ -426,7 +473,7 @@
             rb_copy(1, way).wait_send()
             rb_copy(2, way).wait_send()
 
-    for l in range(3):
+    for l in range(2):
         for step in range(3):
             def done(n):
                 lx_copy(l, step, 0, n).wait_send()
@@ -437,6 +484,11 @@
             lz_copy(l, i).wait_send()
         sent = fin.at[l, pl.ds(1, 19)]
         pltpu.make_async_copy(sent, sent, fin_send.at[l]).wait()
+
+    for way in range(2):
+        for s in range(1, 5):
+            zr_copy(s, way).wait_send()
+    pltpu.make_async_copy(zx, zx, zx_send).wait()
 
     @pl.when(active)
     def _():
@@ -460,7 +512,6 @@
         ),
         in_specs=[
             pl.BlockSpec(memory_space=pl.ANY),
-            pl.BlockSpec(memory_space=pl.ANY),
             pl.BlockSpec(memory_space=pltpu.SMEM),
         ],
         out_specs=(
@@ -470,7 +521,7 @@
         ),
         scratch_shapes=[
             pltpu.VMEM((rows, RB), BF16),
-            pltpu.VMEM((3, NX, NZ, 16, RB), BF16),
+            pltpu.VMEM((2, NX, NZ, 16, RB), BF16),
             pltpu.VMEM((NDP, 4, T, T), F32),
             pltpu.VMEM((NY, 4, T, T), F32),
             pltpu.VMEM((2, 2, T, T), F32),
@@ -483,26 +534,31 @@
             pltpu.VMEM((NDP, CAP * nb, T), F32),
             pltpu.VMEM((NDP, CAP * na, T), F32),
             pltpu.VMEM((NDP, CAP * nb, T), F32),
-            pltpu.VMEM((3, 4, 3, T, T), F32),
-            pltpu.VMEM((3, 2, 3, T // 2, T), F32),
-            pltpu.VMEM((3, 2, 3, T, T), F32),
-            pltpu.VMEM((3, NZ, 4, 16, T), F32),
-            pltpu.VMEM((3, 2, 4, 16, T), F32),
-            pltpu.VMEM((3, 2, 2, 16, T), F32),
-            pltpu.VMEM((3, 20, 16, T), F32),
+            pltpu.VMEM((2, 4, 3, T, T), F32),
+            pltpu.VMEM((2, 2, 3, T // 2, T), F32),
+            pltpu.VMEM((2, 2, 3, T, T), F32),
+            pltpu.VMEM((2, NZ, 4, 16, T), F32),
+            pltpu.VMEM((2, 2, 4, 16, T), F32),
+            pltpu.VMEM((2, 2, 2, 16, T), F32),
+            pltpu.VMEM((2, 20, 16, T), F32),
+            pltpu.VMEM((NZ, 16 * NX, NX * T), F32),
+            pltpu.VMEM((2, 8 * NX, NX * T), F32),
+            pltpu.VMEM((2, 3, 16 * NX, NX * T), F32),
+            pltpu.VMEM((3, 16, NX * T), F32),
             pltpu.VMEM((4 * T, 4 * T), BF16),
             pltpu.VMEM((8, T), jnp.int32),
             pltpu.SMEM((8, T), jnp.int32),
-            dma((8,)), dma,
+            dma((4,)), dma,
             dma((NY,)), dma((NY,)), dma((6,)), dma((6,)),
             dma((2,)), dma((2,)), dma((2, NDP)), dma((2, NDP)),
-            dma((3, 6)), dma((3, 6)), dma((3, 4)), dma((3, 4)), dma((3,)), dma((3,)),
+            dma((2, 6)), dma((2, 6)), dma((2, 4)), dma((2, 4)), dma((2,)), dma((2,)),
+            dma((2, 4)), dma((2, 4)), dma, dma,
         ],
         compiler_params=pltpu.CompilerParams(
             collective_id=0, has_side_effects=True, vmem_limit_bytes=105 * 512 * 1024
         ),
         name="stats",
-    )(gradient, gradient.reshape(3, NZ, NX, 16, RB), owners.reshape(1, NMP))
+    )(gradient, owners.reshape(1, NMP))
     left_stats = BETA * left_old + left_gram
     right_stats = scale[:, None, None] * right_old + right_gram
     return left_stats, right_stats

time: 54 us -> 59.7 us (1.11)
  Pallas kernels: 50.8 us -> 56.6 us
    pallas_call x1, Pallas kernels: 50.8 us -> 56.6 us  [per_device(): pl.pallas_call(kernel, out_shape=(jax.ShapeDtypeStruct((3, 16, 512), F32)...]
where the time goes in v4:
time: 59.7 us; the launch traced here: 59.6 us
  Pallas kernels  56.6 us (95%)
  other arithmetic  1.67 us (3%)
  local copies, waits for them, and re-layouts  0.66 us (1%)
  between operations  0.66 us (1%)
    pallas_call x1, Pallas kernels, per_device(): pl.pallas_call(kernel, out_shape=(jax.ShapeDtypeStruct((3, 16, 512), F32)...  56.6 us

profile of v4, /device:TPU:1, one launch (start us, length us, event | category | flops | bytes accessed | tf_op | source)
XLA Modules:
  0.0 59.6 jit_solution(6225604913179166977)
XLA Ops:
  0.6 0.0 copy-start
  0.6 0.6 %copy-done = s32[32,1]{0,1:T(1,128)S(1)} copy-done((s32[32,1]{0,1:T(1,128)S(1)}, s32[32,1]{0,1:T(1,128)}, u32[]{:S(2)}) %copy-start) | copy-done | bytes 152
  1.3 0.0 copy-start.2
  1.3 0.0 copy-start.1
  1.3 56.6 %stats.1 = (f32[3,16,512]{2,1,0:T(8,128)S(1)}, f32[6,28,896]{2,1,0:T(8,128)S(1)}, f32[6]{0:T(128)S(1)}) custom-call(bf16[1536,896]{1,0:T(8,128)(2,1)} %grad_ref.1, s32[1,32]{1,0:T(1,128)S(1)} %bitcast.1), custom_call_target="tpu_custom_call" | custom-call | tf_op jit(solution)/shard_map/stats/pallas_call | solution.py:506
  57.9 0.0 copy-done.2
  57.9 0.7 %multiply_add_fusion.1 = f32[3,16,512]{2,1,0:T(8,128)} fusion(f32[3,16,512]{2,1,0:T(8,128)S(1)} %get-tuple-element.5, f32[3,16,512]{2,1,0:T(8,128)S(1)} %copy-done.2), kind=kLoop, calls=%fused_computation.1 | loop fusion | flops 49152 | bytes 294912 | tf_op jit(solution)/shard_map/add | solution.py:562
  58.6 0.0 copy-done.1
  58.6 1.0 %multiply_add_fusion = f32[6,28,896]{2,1,0:T(8,128)} fusion(f32[6,28,896]{2,1,0:T(8,128)S(1)} %get-tuple-element.7, f32[6,28,896]{2,1,0:T(8,128)S(1)} %copy-done.1, f32[6]{0:T(128)S(1)} %get-tuple-element.6), kind=kLoop, calls=%fused_computation | loop fusion | flops 301056 | bytes 1806360 | tf_op jit(solution)/shard_map/add | solution.py:563
Async XLA Ops:
  0.6 0.7 %copy-start = (s32[32,1]{0,1:T(1,128)S(1)}, s32[32,1]{0,1:T(1,128)}, u32[]{:S(2)}) copy-start(s32[32,1]{0,1:T(1,128)} %param.5) | copy-start | bytes 388
  1.3 56.6 %copy-start.2 = (f32[3,16,512]{2,1,0:T(8,128)S(1)}, f32[3,16,512]{2,1,0:T(8,128)}, u32[]{:S(2)}) copy-start(f32[3,16,512]{2,1,0:T(8,128)} %param.6) | copy-start | bytes 294916
  1.3 57.3 %copy-start.1 = (f32[6,28,896]{2,1,0:T(8,128)S(1)}, f32[6,28,896]{2,1,0:T(8,128)}, u32[]{:S(2)}) copy-start(f32[6,28,896]{2,1,0:T(8,128)} %param.7) | copy-start | bytes 1806340

commit v5 on v4

--- a/solution.py
+++ b/solution.py
@@ -41,9 +41,9 @@
 
 
 def kernel(
-    grad_ref, owners_ref, left_ref, right_ref, scale_ref,
+    grad_ref, owners_ref, left_ref, right_ref,
     h, a, part, ra, rb1, rb2, tall, t28, r2a, r2b, s3a, s3b, r3a, r3b,
-    lp, lx1, lx2, lz, rly, rlyh, fin, zg, zr1, zr2, zx, perm, tabv, tab,
+    lp, lx1, lx2, lz, rly, rlyh, fin, zg, zr, zx, perm, own, tabv, tab,
     in_sem, tab_sem, ra_send, ra_recv, rb_send, rb_recv,
     r2_send, r2_recv, r3_send, r3_recv,
     lx_send, lx_recv, lz_send, lz_recv, fin_send, fin_recv,
@@ -62,13 +62,13 @@
     def has(q, core):
         return 2 * q + core < NT
 
-    rows = h.shape[0]
-    load_h = []
-    for i in range(4):
-        n = rows // 4
-        cp = pltpu.make_async_copy(grad_ref.at[pl.ds(i * n, n)], h.at[pl.ds(i * n, n)], in_sem.at[i])
-        cp.start()
-        load_h.append(cp)
+    nb = NX * T
+    load_h = {}
+    for l in (2, 0, 1):
+        load_h[l] = pltpu.make_async_copy(grad_ref.at[pl.ds(l * nb, nb)], h.at[pl.ds(l * nb, nb)], in_sem.at[l])
+        load_h[l].start()
+    load_owners = pltpu.make_async_copy(owners_ref, own, in_sem.at[3])
+    load_owners.start()
 
     barrier = pltpu.get_barrier_semaphore()
 
@@ -83,11 +83,12 @@
     lax.fori_loop(1, NDP, hello_dp, 0)
     lax.fori_loop(1, NMP, hello_mp, 0)
 
-    def right_part(q):
+    def right_part(l, q):
         lo = 2 * T * q
         wide = min(2 * T, RB - lo)
+        some = slice(l * nb, (l + 1) * nb)
         block = lax.dot_general(
-            h[:, lo:RB], h[:, lo:lo + wide], (((0,), (0,)), ((), ())), preferred_element_type=F32
+            h[some, lo:RB], h[some, lo:lo + wide], (((0,), (0,)), ((), ())), preferred_element_type=F32
         )
         for col in range(2 * q, 2 * q + wide // T):
             for row in range(col, NT):
@@ -95,7 +96,8 @@
                 u = (4 * d) % NT
                 k = min((row - u) % NT, (u - row) % NT)
                 i, j = (row - 2 * q) * T, (col - 2 * q) * T
-                part[d, k] = block[i:i + T, j:j + T]
+                tile = block[i:i + T, j:j + T]
+                part[d, k] = tile if l == 2 else part[d, k] + tile
 
     order = [(y + k) % NY for k in (2, 1, 3, 0)]
     q2, q1, q3, q0 = order
@@ -167,12 +169,9 @@
 
         @pl.when(active)
         def _():
-            def go(i, carry):
+            for i in range(1, NMP):
                 to = (mp + i) % NMP
                 remote(t28.at[to, pl.ds(lo, n)], r2.at[NMP - i], r2_send.at[k], r2_recv.at[k], dp, to).start()
-                return carry
-
-            lax.fori_loop(1, NMP, go, 0)
             r2[0] = t28[mp, lo:lo + n]
 
     def r3_copy(k, i):
@@ -327,31 +326,26 @@
         block = lax.dot_general(g, g, (((1,), (1,)), ((), ())), preferred_element_type=F32)
         zg[...] = block.reshape(NZ, 16 * NX, NX * T)
 
-    def zr_copy(s, way):
+    def zr_copy(s, way, late):
         sign = 1 - 2 * way
-        src = zg.at[zz(sign * (5 - s))]
-        if s == 1:
-            src, dst = zg.at[zz(4), pl.ds(way * zh, zh)], zr1.at[way]
-        else:
-            dst = zr2.at[way, s - 2]
-        return remote(src, dst, zr_send.at[way, s - 1], zr_recv.at[way, s - 1], dp, zz(sign) * NX + x)
-
-    def zr_start(s):
+        cut = pl.ds((1 - way if late else way) * zh, zh)
+        i = s + 2 if late else s - 1
+        src = zg.at[zz(sign * (5 - s)), cut]
+        return remote(src, zr.at[way, i], zr_send.at[way, i], zr_recv.at[way, i], dp, zz(sign) * NX + x)
+
+    def zr_start(s, late):
         for way in range(2):
-            zr_copy(s, way).start()
-
-    def zr_next(s):
+            zr_copy(s, way, late).start()
+
+    def zr_next(s, late):
         for way in range(2):
             sign = 1 - 2 * way
             t = zz(sign * (4 - s))
-            zr_copy(s, way).wait_recv()
-            if s == 1:
-                cut = slice(way * zh, (way + 1) * zh)
-                zg[t, cut] = zg[t, cut] + zr1[way]
-            else:
-                zg[t] = zg[t] + zr2[way, s - 2]
+            lo = (1 - way if late else way) * zh
+            zr_copy(s, way, late).wait_recv()
+            zg[t, lo:lo + zh] = zg[t, lo:lo + zh] + zr[way, s + 2 if late else s - 1]
             if s < 4:
-                zr_copy(s + 1, way).start()
+                zr_copy(s + 1, way, late).start()
 
     def x_rows(to):
         return pl.ds(pl.multiple_of(16 * to, 16), 16)
@@ -372,6 +366,7 @@
         perm[...] = (place == q).astype(F32).astype(BF16)
 
     def make_table():
+        load_owners.wait()
         lane = lax.broadcasted_iota(jnp.int32, (8, T), 1)
         lane_owner = (lane * 43) >> 8
         lane_rank = lane - lane_owner * CAP
@@ -379,7 +374,7 @@
         found = jnp.zeros((8, T), jnp.int32)
         mine = jnp.int32(0)
         for b in range(NMP):
-            o = owners_ref[0, b]
+            o = own[0, b]
             same = lane_owner == o
             found = jnp.where(same & (seen == lane_rank), b, found)
             seen = seen + same.astype(jnp.int32)
@@ -388,12 +383,9 @@
         cp = pltpu.make_async_copy(tabv, tab, tab_sem)
         cp.start()
         cp.wait()
-        valid = [(k < mine).astype(F32) for k in range(CAP)]
-        for k in range(CAP):
-            scale_ref[k] = BETA * valid[k]
-        return valid
-
-    def right_out(k, valid):
+        return [jnp.where(k < mine, F32(0), F32(jnp.nan)) for k in range(CAP)]
+
+    def right_out(k, empty):
         lo, n = CHUNK[k]
         r3 = (r3a, r3b)[k]
         for d in range(NT):
@@ -411,17 +403,18 @@
             for s in range(CAP):
                 cut = slice(n * s, n * (s + 1))
                 value = jnp.where(upper, r3[one, cut, :], r3[two, cut, :])
-                right_ref[s, lo:lo + n, g * T:(g + 1) * T] = value * valid[s]
-
-    for cp in load_h:
-        cp.wait()
-    for q in range(4):
-        right_part(q)
+                right_ref[s, lo:lo + n, g * T:(g + 1) * T] = value + empty[s]
+
+    for l in (2, 0, 1):
+        load_h[l].wait()
+        for q in range(4):
+            right_part(l, q)
     pl.semaphore_wait(barrier, NMP - 1 + NDP - 1)
     for i in range(4):
         ra_go(i)
     z_part()
-    zr_start(1)
+    zr_start(1, False)
+    zr_start(2, True)
     left_part(0)
     lx_start(0, 0)
     lx_start(0, 1)
@@ -429,33 +422,36 @@
     ra_sum(1)
     ra_sum(2)
     left_part(1)
+    zr_next(1, False)
+    lx_second(0)
     lx_start(1, 0)
     lx_start(1, 1)
+    zr_next(2, True)
     ra_sum(3)
-    valid = make_table()
-    zr_next(1)
-    lx_second(0)
+    empty = make_table()
     rb_second()
+    zr_next(2, False)
+    zr_next(3, True)
+    lz_first(0)
+    zr_next(3, False)
     lx_second(1)
-    make_perm()
-    zr_next(2)
-    lz_first(0)
+    zr_next(4, True)
     right_whole()
     r2_go(0)
+    lz_second(0)
+    zr_next(4, False)
+    zx_start()
     r2_go(1)
-    zr_next(3)
-    lz_second(0)
     lz_first(1)
-    zr_next(4)
-    zx_start()
-    lz_second(1)
+    make_perm()
+    lz_last(0)
     r3_go(0)
-    lz_last(0)
-    lz_last(1)
     zx_last()
     r3_go(1)
-    right_out(0, valid)
-    right_out(1, valid)
+    lz_second(1)
+    right_out(0, empty)
+    lz_last(1)
+    right_out(1, empty)
 
     for i in range(NY):
         @pl.when(has(order[i], other))
@@ -487,7 +483,9 @@
 
     for way in range(2):
         for s in range(1, 5):
-            zr_copy(s, way).wait_send()
+            zr_copy(s, way, False).wait_send()
+            if s > 1:
+                zr_copy(s, way, True).wait_send()
     pltpu.make_async_copy(zx, zx, zx_send).wait()
 
     @pl.when(active)
@@ -503,21 +501,19 @@
     rows = gradient.shape[0]
     dma = pltpu.SemaphoreType.DMA
     na, nb = CHUNK[0][1], CHUNK[1][1]
-    left_gram, right_gram, scale = pl.pallas_call(
+    left_gram, right_gram = pl.pallas_call(
         kernel,
         out_shape=(
             jax.ShapeDtypeStruct((3, 16, 512), F32),
             jax.ShapeDtypeStruct((CAP, RPM, RB), F32),
-            jax.ShapeDtypeStruct((CAP,), F32),
         ),
         in_specs=[
             pl.BlockSpec(memory_space=pl.ANY),
-            pl.BlockSpec(memory_space=pltpu.SMEM),
+            pl.BlockSpec(memory_space=pl.ANY),
         ],
         out_specs=(
             pl.BlockSpec(memory_space=pltpu.VMEM),
             pl.BlockSpec(memory_space=pltpu.VMEM),
-            pl.BlockSpec(memory_space=pltpu.SMEM),
         ),
         scratch_shapes=[
             pltpu.VMEM((rows, RB), BF16),
@@ -542,17 +538,17 @@
             pltpu.VMEM((2, 2, 2, 16, T), F32),
             pltpu.VMEM((2, 20, 16, T), F32),
             pltpu.VMEM((NZ, 16 * NX, NX * T), F32),
-            pltpu.VMEM((2, 8 * NX, NX * T), F32),
-            pltpu.VMEM((2, 3, 16 * NX, NX * T), F32),
+            pltpu.VMEM((2, 7, 8 * NX, NX * T), F32),
             pltpu.VMEM((3, 16, NX * T), F32),
             pltpu.VMEM((4 * T, 4 * T), BF16),
+            pltpu.SMEM((1, NMP), jnp.int32),
             pltpu.VMEM((8, T), jnp.int32),
             pltpu.SMEM((8, T), jnp.int32),
             dma((4,)), dma,
             dma((NY,)), dma((NY,)), dma((6,)), dma((6,)),
             dma((2,)), dma((2,)), dma((2, NDP)), dma((2, NDP)),
             dma((2, 6)), dma((2, 6)), dma((2, 4)), dma((2, 4)), dma((2,)), dma((2,)),
-            dma((2, 4)), dma((2, 4)), dma, dma,
+            dma((2, 7)), dma((2, 7)), dma, dma,
         ],
         compiler_params=pltpu.CompilerParams(
             collective_id=0, has_side_effects=True, vmem_limit_bytes=105 * 512 * 1024
@@ -560,7 +556,7 @@
         name="stats",
     )(gradient, owners.reshape(1, NMP))
     left_stats = BETA * left_old + left_gram
-    right_stats = scale[:, None, None] * right_old + right_gram
+    right_stats = jnp.where(jnp.isnan(right_gram), 0.0, BETA * right_old + right_gram)
     return left_stats, right_stats
 
 

time: 59.7 us -> 52 us (0.87)
  Pallas kernels: 56.6 us -> 49 us
    pallas_call x1, Pallas kernels: 56.6 us -> 49 us  [per_device(): pl.pallas_call(kernel, out_shape=(jax.ShapeDtypeStruct((3, 16, 512), F32)...]
    add x1 -> x0, other arithmetic: 1.01 us -> none  [per_device(): right_stats = scale[:, None, None] * right_old + right_gram]
    select_n x0 -> x1, other arithmetic: none -> 0.94 us  [per_device(): jnp.where(jnp.isnan(right_gram), 0.0, BETA * right_old + right_gram)]
where the time goes in v5:
time: 52 us; the launch traced here: 51.9 us
  Pallas kernels  49 us (94%)
  other arithmetic  1.6 us (3%)
  local copies, waits for them, and re-layouts  0.66 us (1%)
  between operations  0.66 us (1%)
    pallas_call x1, Pallas kernels, per_device(): pl.pallas_call(kernel, out_shape=(jax.ShapeDtypeStruct((3, 16, 512), F32)...  49 us

profile of v5, /device:TPU:1, one launch (start us, length us, event | category | flops | bytes accessed | tf_op | source)
XLA Modules:
  0.0 51.9 jit_solution(2385375763649639728)
XLA Ops:
  0.6 0.0 copy-start
  0.6 0.6 %copy-done = s32[32,1]{0,1:T(1,128)S(1)} copy-done((s32[32,1]{0,1:T(1,128)S(1)}, s32[32,1]{0,1:T(1,128)}, u32[]{:S(2)}) %copy-start) | copy-done | bytes 152
  1.3 0.0 copy-start.2
  1.3 0.0 copy-start.1
  1.3 49.0 %stats.1 = (f32[3,16,512]{2,1,0:T(8,128)S(1)}, f32[6,28,896]{2,1,0:T(8,128)S(1)}) custom-call(bf16[1536,896]{1,0:T(8,128)(2,1)} %grad_ref.1, s32[1,32]{1,0:T(1,128)S(1)} %bitcast.1), custom_call_target="tpu_custom_call" | custom-call | tf_op jit(solution)/shard_map/stats/pallas_call | solution.py:504
  50.3 0.0 copy-done.2
  50.3 0.7 %multiply_add_fusion = f32[3,16,512]{2,1,0:T(8,128)} fusion(f32[3,16,512]{2,1,0:T(8,128)S(1)} %get-tuple-element.4, f32[3,16,512]{2,1,0:T(8,128)S(1)} %copy-done.2), kind=kLoop, calls=%fused_computation.1 | loop fusion | flops 49152 | bytes 294912 | tf_op jit(solution)/shard_map/add | solution.py:558
  50.9 0.0 copy-done.1
  50.9 0.9 %add_select_fusion = f32[6,28,896]{2,1,0:T(8,128)} fusion(f32[6,28,896]{2,1,0:T(8,128)S(1)} %get-tuple-element.5, f32[6,28,896]{2,1,0:T(8,128)S(1)} %copy-done.1), kind=kLoop, calls=%fused_computation | loop fusion | flops 602112 | bytes 1806336 | tf_op jit(solution)/shard_map/jit(_where)/select_n | solution.py:559
Async XLA Ops:
  0.6 0.7 %copy-start = (s32[32,1]{0,1:T(1,128)S(1)}, s32[32,1]{0,1:T(1,128)}, u32[]{:S(2)}) copy-start(s32[32,1]{0,1:T(1,128)} %param.5) | copy-start | bytes 388
  1.3 49.0 %copy-start.2 = (f32[3,16,512]{2,1,0:T(8,128)S(1)}, f32[3,16,512]{2,1,0:T(8,128)}, u32[]{:S(2)}) copy-start(f32[3,16,512]{2,1,0:T(8,128)} %param.6) | copy-start | bytes 294916
  1.3 49.7 %copy-start.1 = (f32[6,28,896]{2,1,0:T(8,128)S(1)}, f32[6,28,896]{2,1,0:T(8,128)}, u32[]{:S(2)}) copy-start(f32[6,28,896]{2,1,0:T(8,128)} %param.7) | copy-start | bytes 1806340

commit v6 on v5

--- a/solution.py
+++ b/solution.py
@@ -247,24 +247,24 @@
     def zz(k):
         return (z + NZ + k) % NZ
 
-    def lz_copy(l, i):
+    def lz_copy(i):
         to, src, dst = (
-            (1, lz.at[l, zz(3)], rly.at[l, 0]),
-            (-1, lz.at[l, zz(-3)], rly.at[l, 1]),
-            (2, lz.at[l, zz(4), pl.ds(0, 2)], rlyh.at[l, 0]),
-            (-2, lz.at[l, zz(4), pl.ds(2, 2)], rlyh.at[l, 1]),
+            (1, lz.at[zz(3)], rly.at[0]),
+            (-1, lz.at[zz(-3)], rly.at[1]),
+            (2, lz.at[zz(4), pl.ds(0, 2)], rlyh.at[0]),
+            (-2, lz.at[zz(4), pl.ds(2, 2)], rlyh.at[1]),
         )[i]
-        return remote(src, dst, lz_send.at[l, i], lz_recv.at[l, i], dp, zz(to) * NX + x)
+        return remote(src, dst, lz_send.at[i], lz_recv.at[i], dp, zz(to) * NX + x)
 
     hops = (0, 1, -1, 2, -2)
 
-    def fin_start(l, j):
+    def fin_start(j):
         for r in range(0 if j else 1, 4):
             g = (x + 4 - r) % 4
             to = zz(hops[j])
-            remote(lz.at[l, to, g], fin.at[l, 4 * j + r], fin_send.at[l], fin_recv.at[l], dp, to * NX + g).start()
-
-    def lz_first(l):
+            remote(lz.at[to, g], fin.at[4 * j + r], fin_send, fin_recv, dp, to * NX + g).start()
+
+    def lz_put(l):
         def go(n):
             for way in range(2):
                 lx_copy(l, 1, way, n).wait_recv()
@@ -273,7 +273,7 @@
             tiles = [lp[l, v, i] + lx2[l, 0, i] + lx2[l, 1, i] for i in range(n)]
 
             def put(g, tile):
-                lz[l, :, g] = tile.reshape(NZ, 16, T)
+                lz[:, g, l] = tile.reshape(NZ, 16, T)
 
             if n == 3:
                 w = v // 2
@@ -288,36 +288,42 @@
                 put((v + 2) % 4, tiles[1].T)
 
         by_parity(x + 4 - l, go)
+
+    def lz_first():
         for i in (2, 3, 0, 1):
-            lz_copy(l, i).start()
+            lz_copy(i).start()
         for j in (1, 2, 0):
-            fin_start(l, j)
-        fin[l, 0] = lz[l, z, x]
-
-    def lz_second(l):
+            fin_start(j)
+        fin[0] = lz[z, x]
+
+    def lz_second():
         for way in range(2):
             t = (zz(2), zz(-2))[way]
-            lz_copy(l, way).wait_recv()
-            lz_copy(l, 2 + way).wait_recv()
-            lz[l, t] = lz[l, t] + rly[l, way]
-            lz[l, t, 2 * way:2 * way + 2] = lz[l, t, 2 * way:2 * way + 2] + rlyh[l, way]
-            fin_start(l, 3 + way)
-
-    def lz_last(l):
-        everything = fin.at[l, pl.ds(1, 19)]
-        pltpu.make_async_copy(everything, everything, fin_recv.at[l]).wait()
-        row = []
-        for g in range(4):
-            r = (g + l) % 4
-            row.append(fin[l, r] + fin[l, 4 + r] + fin[l, 8 + r] + fin[l, 12 + r] + fin[l, 16 + r])
-        row = jnp.concatenate(row, axis=1)
+            lz_copy(way).wait_recv()
+            lz_copy(2 + way).wait_recv()
+            lz[t] = lz[t] + rly[way]
+            lz[t, 2 * way:2 * way + 2] = lz[t, 2 * way:2 * way + 2] + rlyh[way]
+            fin_start(3 + way)
+
+    def lz_last():
+        everything = fin.at[pl.ds(1, 19)]
+        pltpu.make_async_copy(everything, everything, fin_recv).wait()
+        rows = []
+        for l in range(2):
+            row = []
+            for g in range(4):
+                r = (g + l) % 4
+                row.append(fin[r, l] + fin[4 + r, l] + fin[8 + r, l] + fin[12 + r, l] + fin[16 + r, l])
+            rows.append(jnp.concatenate(row, axis=1))
+        rows = jnp.concatenate(rows, axis=0)
         total = None
         for _ in range(3):
-            piece = row.astype(BF16)
-            row = row - piece.astype(F32)
+            piece = rows.astype(BF16)
+            rows = rows - piece.astype(F32)
             term = jnp.dot(piece, perm[...], preferred_element_type=F32)
             total = term if total is None else total + term
-        left_ref[l] = total
+        left_ref[0] = total[:16]
+        left_ref[1] = total[16:]
 
     zh = 8 * NX
 
@@ -404,6 +410,51 @@
                 cut = slice(n * s, n * (s + 1))
                 value = jnp.where(upper, r3[one, cut, :], r3[two, cut, :])
                 right_ref[s, lo:lo + n, g * T:(g + 1) * T] = value + empty[s]
+
+    def sent_early():
+        for i in range(NY):
+            @pl.when(has(order[i], other))
+            def _():
+                ra_copy(i).wait_send()
+
+        @pl.when(has(q2, c))
+        def _():
+            rb_copy(0, 0).wait_send()
+            rb_copy(0, 1).wait_send()
+
+        for way in range(2):
+            @pl.when(has((q1, q3)[way], c))
+            def _():
+                rb_copy(1, way).wait_send()
+                rb_copy(2, way).wait_send()
+
+        for l in range(2):
+            for step in range(3):
+                def done(n):
+                    lx_copy(l, step, 0, n).wait_send()
+                    lx_copy(l, step, 1, n).wait_send()
+
+                by_parity(x + 4 - l + (0 if step == 0 else 1), done)
+        for way in range(2):
+            for s in range(1, 5):
+                zr_copy(s, way, False).wait_send()
+                if s > 1:
+                    zr_copy(s, way, True).wait_send()
+
+    def sent_late():
+        for i in range(4):
+            lz_copy(i).wait_send()
+        sent = fin.at[pl.ds(1, 19)]
+        pltpu.make_async_copy(sent, sent, fin_send).wait()
+        pltpu.make_async_copy(zx, zx, zx_send).wait()
+
+        @pl.when(active)
+        def _():
+            for k in range(2):
+                sent = (r2a, r2b)[k].at[pl.ds(1, NMP - 1)]
+                pltpu.make_async_copy(sent, sent, r2_send.at[k]).wait()
+                for i in range(1, NDP):
+                    r3_copy(k, i).wait_send()
 
     for l in (2, 0, 1):
         load_h[l].wait()
@@ -432,69 +483,27 @@
     rb_second()
     zr_next(2, False)
     zr_next(3, True)
-    lz_first(0)
+    lz_put(0)
     zr_next(3, False)
     lx_second(1)
-    zr_next(4, True)
     right_whole()
     r2_go(0)
-    lz_second(0)
+    zr_next(4, True)
     zr_next(4, False)
     zx_start()
+    lz_put(1)
     r2_go(1)
-    lz_first(1)
+    lz_first()
     make_perm()
-    lz_last(0)
+    sent_early()
+    zx_last()
     r3_go(0)
-    zx_last()
+    lz_second()
     r3_go(1)
-    lz_second(1)
     right_out(0, empty)
-    lz_last(1)
+    lz_last()
     right_out(1, empty)
-
-    for i in range(NY):
-        @pl.when(has(order[i], other))
-        def _():
-            ra_copy(i).wait_send()
-
-    @pl.when(has(q2, c))
-    def _():
-        rb_copy(0, 0).wait_send()
-        rb_copy(0, 1).wait_send()
-
-    for way in range(2):
-        @pl.when(has((q1, q3)[way], c))
-        def _():
-            rb_copy(1, way).wait_send()
-            rb_copy(2, way).wait_send()
-
-    for l in range(2):
-        for step in range(3):
-            def done(n):
-                lx_copy(l, step, 0, n).wait_send()
-                lx_copy(l, step, 1, n).wait_send()
-
-            by_parity(x + 4 - l + (0 if step == 0 else 1), done)
-        for i in range(4):
-            lz_copy(l, i).wait_send()
-        sent = fin.at[l, pl.ds(1, 19)]
-        pltpu.make_async_copy(sent, sent, fin_send.at[l]).wait()
-
-    for way in range(2):
-        for s in range(1, 5):
-            zr_copy(s, way, False).wait_send()
-            if s > 1:
-                zr_copy(s, way, True).wait_send()
-    pltpu.make_async_copy(zx, zx, zx_send).wait()
-
-    @pl.when(active)
-    def _():
-        for k in range(2):
-            sent = (r2a, r2b)[k].at[pl.ds(1, NMP - 1)]
-            pltpu.make_async_copy(sent, sent, r2_send.at[k]).wait()
-            for i in range(1, NDP):
-                r3_copy(k, i).wait_send()
+    sent_late()
 
 
 def per_device(gradient, owners, left_old, right_old):
@@ -533,10 +542,10 @@
             pltpu.VMEM((2, 4, 3, T, T), F32),
             pltpu.VMEM((2, 2, 3, T // 2, T), F32),
             pltpu.VMEM((2, 2, 3, T, T), F32),
-            pltpu.VMEM((2, NZ, 4, 16, T), F32),
-            pltpu.VMEM((2, 2, 4, 16, T), F32),
+            pltpu.VMEM((NZ, 4, 2, 16, T), F32),
+            pltpu.VMEM((2, 4, 2, 16, T), F32),
             pltpu.VMEM((2, 2, 2, 16, T), F32),
-            pltpu.VMEM((2, 20, 16, T), F32),
+            pltpu.VMEM((20, 2, 16, T), F32),
             pltpu.VMEM((NZ, 16 * NX, NX * T), F32),
             pltpu.VMEM((2, 7, 8 * NX, NX * T), F32),
             pltpu.VMEM((3, 16, NX * T), F32),
@@ -547,7 +556,7 @@
             dma((4,)), dma,
             dma((NY,)), dma((NY,)), dma((6,)), dma((6,)),
             dma((2,)), dma((2,)), dma((2, NDP)), dma((2, NDP)),
-            dma((2, 6)), dma((2, 6)), dma((2, 4)), dma((2, 4)), dma((2,)), dma((2,)),
+            dma((2, 6)), dma((2, 6)), dma((4,)), dma((4,)), dma, dma,
             dma((2, 7)), dma((2, 7)), dma, dma,
         ],
         compiler_params=pltpu.CompilerParams(

time: 52 us -> 50 us (0.962)
  Pallas kernels: 49 us -> 47 us
    pallas_call x1, Pallas kernels: 49 us -> 47 us  [per_device(): pl.pallas_call(kernel, out_shape=(jax.ShapeDtypeStruct((3, 16, 512), F32)...]
where the time goes in v6:
time: 50 us; the launch traced here: 49.9 us
  Pallas kernels  47 us (94%)
  other arithmetic  1.6 us (3%)
  local copies, waits for them, and re-layouts  0.66 us (1%)
  between operations  0.66 us (1%)
    pallas_call x1, Pallas kernels, per_device(): pl.pallas_call(kernel, out_shape=(jax.ShapeDtypeStruct((3, 16, 512), F32)...  47 us

profile of v6, /device:TPU:1, one launch (start us, length us, event | category | flops | bytes accessed | tf_op | source)
XLA Modules:
  0.0 49.9 jit_solution(7032241251437774256)
XLA Ops:
  0.6 0.0 copy-start
  0.6 0.6 %copy-done = s32[32,1]{0,1:T(1,128)S(1)} copy-done((s32[32,1]{0,1:T(1,128)S(1)}, s32[32,1]{0,1:T(1,128)}, u32[]{:S(2)}) %copy-start) | copy-done | bytes 152
  1.3 0.0 copy-start.2
  1.3 0.0 copy-start.1
  1.3 47.0 %stats.1 = (f32[3,16,512]{2,1,0:T(8,128)S(1)}, f32[6,28,896]{2,1,0:T(8,128)S(1)}) custom-call(bf16[1536,896]{1,0:T(8,128)(2,1)} %grad_ref.1, s32[1,32]{1,0:T(1,128)S(1)} %bitcast.1), custom_call_target="tpu_custom_call" | custom-call | tf_op jit(solution)/shard_map/stats/pallas_call | solution.py:513
  48.3 0.0 copy-done.2
  48.3 0.7 %multiply_add_fusion = f32[3,16,512]{2,1,0:T(8,128)} fusion(f32[3,16,512]{2,1,0:T(8,128)S(1)} %get-tuple-element.4, f32[3,16,512]{2,1,0:T(8,128)S(1)} %copy-done.2), kind=kLoop, calls=%fused_computation.1 | loop fusion | flops 49152 | bytes 294912 | tf_op jit(solution)/shard_map/add | solution.py:567
  49.0 0.0 copy-done.1
  49.0 0.9 %add_select_fusion = f32[6,28,896]{2,1,0:T(8,128)} fusion(f32[6,28,896]{2,1,0:T(8,128)S(1)} %get-tuple-element.5, f32[6,28,896]{2,1,0:T(8,128)S(1)} %copy-done.1), kind=kLoop, calls=%fused_computation | loop fusion | flops 602112 | bytes 1806336 | tf_op jit(solution)/shard_map/jit(_where)/select_n | solution.py:568
Async XLA Ops:
  0.6 0.7 %copy-start = (s32[32,1]{0,1:T(1,128)S(1)}, s32[32,1]{0,1:T(1,128)}, u32[]{:S(2)}) copy-start(s32[32,1]{0,1:T(1,128)} %param.5) | copy-start | bytes 388
  1.3 47.0 %copy-start.2 = (f32[3,16,512]{2,1,0:T(8,128)S(1)}, f32[3,16,512]{2,1,0:T(8,128)}, u32[]{:S(2)}) copy-start(f32[3,16,512]{2,1,0:T(8,128)} %param.6) | copy-start | bytes 294916
  1.3 47.7 %copy-start.1 = (f32[6,28,896]{2,1,0:T(8,128)S(1)}, f32[6,28,896]{2,1,0:T(8,128)}, u32[]{:S(2)}) copy-start(f32[6,28,896]{2,1,0:T(8,128)} %param.7) | copy-start | bytes 1806340

commit v7 on v6

--- a/solution.py
+++ b/solution.py
@@ -441,11 +441,9 @@
                 if s > 1:
                     zr_copy(s, way, True).wait_send()
 
-    def sent_late():
+    def sent_next():
         for i in range(4):
             lz_copy(i).wait_send()
-        sent = fin.at[pl.ds(1, 19)]
-        pltpu.make_async_copy(sent, sent, fin_send).wait()
         pltpu.make_async_copy(zx, zx, zx_send).wait()
 
         @pl.when(active)
@@ -453,8 +451,17 @@
             for k in range(2):
                 sent = (r2a, r2b)[k].at[pl.ds(1, NMP - 1)]
                 pltpu.make_async_copy(sent, sent, r2_send.at[k]).wait()
-                for i in range(1, NDP):
-                    r3_copy(k, i).wait_send()
+            for i in range(1, NDP):
+                r3_copy(0, i).wait_send()
+
+    def sent_late():
+        sent = fin.at[pl.ds(1, 19)]
+        pltpu.make_async_copy(sent, sent, fin_send).wait()
+
+        @pl.when(active)
+        def _():
+            for i in range(1, NDP):
+                r3_copy(1, i).wait_send()
 
     for l in (2, 0, 1):
         load_h[l].wait()
@@ -472,35 +479,36 @@
     ra_sum(0)
     ra_sum(1)
     ra_sum(2)
+    zr_next(1, False)
     left_part(1)
-    zr_next(1, False)
     lx_second(0)
     lx_start(1, 0)
     lx_start(1, 1)
     zr_next(2, True)
     ra_sum(3)
-    empty = make_table()
     rb_second()
     zr_next(2, False)
     zr_next(3, True)
     lz_put(0)
     zr_next(3, False)
     lx_second(1)
+    empty = make_table()
+    make_perm()
     right_whole()
     r2_go(0)
     zr_next(4, True)
     zr_next(4, False)
     zx_start()
+    r2_go(1)
     lz_put(1)
-    r2_go(1)
     lz_first()
-    make_perm()
+    r3_go(0)
     sent_early()
     zx_last()
-    r3_go(0)
+    r3_go(1)
     lz_second()
-    r3_go(1)
     right_out(0, empty)
+    sent_next()
     lz_last()
     right_out(1, empty)
     sent_late()

time: 50 us -> 49.4 us (0.988)
  Pallas kernels: 47 us -> 46.2 us
    pallas_call x1, Pallas kernels: 47 us -> 46.2 us  [per_device(): pl.pallas_call(kernel, out_shape=(jax.ShapeDtypeStruct((3, 16, 512), F32)...]
where the time goes in v7:
time: 49.4 us; the launch traced here: 49.1 us
  Pallas kernels  46.2 us (94%)
  other arithmetic  1.6 us (3%)
  local copies, waits for them, and re-layouts  0.66 us (1%)
  between operations  0.66 us (1%)
    pallas_call x1, Pallas kernels, per_device(): pl.pallas_call(kernel, out_shape=(jax.ShapeDtypeStruct((3, 16, 512), F32)...  46.2 us

profile of v7, /device:TPU:1, one launch (start us, length us, event | category | flops | bytes accessed | tf_op | source)
XLA Modules:
  0.0 49.1 jit_solution(15900813777384889782)
XLA Ops:
  0.6 0.0 copy-start
  0.6 0.6 %copy-done = s32[32,1]{0,1:T(1,128)S(1)} copy-done((s32[32,1]{0,1:T(1,128)S(1)}, s32[32,1]{0,1:T(1,128)}, u32[]{:S(2)}) %copy-start) | copy-done | bytes 152
  1.3 0.0 copy-start.2
  1.3 0.0 copy-start.1
  1.3 46.2 %stats.1 = (f32[3,16,512]{2,1,0:T(8,128)S(1)}, f32[6,28,896]{2,1,0:T(8,128)S(1)}) custom-call(bf16[1536,896]{1,0:T(8,128)(2,1)} %grad_ref.1, s32[1,32]{1,0:T(1,128)S(1)} %bitcast.1), custom_call_target="tpu_custom_call" | custom-call | tf_op jit(solution)/shard_map/stats/pallas_call | solution.py:521
  47.5 0.0 copy-done.2
  47.5 0.7 %multiply_add_fusion = f32[3,16,512]{2,1,0:T(8,128)} fusion(f32[3,16,512]{2,1,0:T(8,128)S(1)} %get-tuple-element.4, f32[3,16,512]{2,1,0:T(8,128)S(1)} %copy-done.2), kind=kLoop, calls=%fused_computation.1 | loop fusion | flops 49152 | bytes 294912 | tf_op jit(solution)/shard_map/add | solution.py:575
  48.1 0.0 copy-done.1
  48.1 0.9 %add_select_fusion = f32[6,28,896]{2,1,0:T(8,128)} fusion(f32[6,28,896]{2,1,0:T(8,128)S(1)} %get-tuple-element.5, f32[6,28,896]{2,1,0:T(8,128)S(1)} %copy-done.1), kind=kLoop, calls=%fused_computation | loop fusion | flops 602112 | bytes 1806336 | tf_op jit(solution)/shard_map/jit(_where)/select_n | solution.py:576
Async XLA Ops:
  0.6 0.7 %copy-start = (s32[32,1]{0,1:T(1,128)S(1)}, s32[32,1]{0,1:T(1,128)}, u32[]{:S(2)}) copy-start(s32[32,1]{0,1:T(1,128)} %param.5) | copy-start | bytes 388
  1.3 46.2 %copy-start.2 = (f32[3,16,512]{2,1,0:T(8,128)S(1)}, f32[3,16,512]{2,1,0:T(8,128)}, u32[]{:S(2)}) copy-start(f32[3,16,512]{2,1,0:T(8,128)} %param.6) | copy-start | bytes 294916
  1.3 46.9 %copy-start.1 = (f32[6,28,896]{2,1,0:T(8,128)S(1)}, f32[6,28,896]{2,1,0:T(8,128)}, u32[]{:S(2)}) copy-start(f32[6,28,896]{2,1,0:T(8,128)} %param.7) | copy-start | bytes 1806340

commit v8 on v7

--- a/solution.py
+++ b/solution.py
@@ -504,8 +504,8 @@
     lz_first()
     r3_go(0)
     sent_early()
+    r3_go(1)
     zx_last()
-    r3_go(1)
     lz_second()
     right_out(0, empty)
     sent_next()

time: 49.4 us -> 49.4 us (level)
  no operation moved by 1% of the time
where the time goes in v8:
time: 49.4 us; the launch traced here: 49.1 us
  Pallas kernels  46.2 us (94%)
  other arithmetic  1.6 us (3%)
  local copies, waits for them, and re-layouts  0.66 us (1%)
  between operations  0.66 us (1%)
    pallas_call x1, Pallas kernels, per_device(): pl.pallas_call(kernel, out_shape=(jax.ShapeDtypeStruct((3, 16, 512), F32)...  46.2 us

profile of v8, /device:TPU:1, one launch (start us, length us, event | category | flops | bytes accessed | tf_op | source)
XLA Modules:
  0.0 49.1 jit_solution(16013245079357810277)
XLA Ops:
  0.6 0.0 copy-start
  0.6 0.6 %copy-done = s32[32,1]{0,1:T(1,128)S(1)} copy-done((s32[32,1]{0,1:T(1,128)S(1)}, s32[32,1]{0,1:T(1,128)}, u32[]{:S(2)}) %copy-start) | copy-done | bytes 152
  1.3 0.0 copy-start.2
  1.3 0.0 copy-start.1
  1.3 46.2 %stats.1 = (f32[3,16,512]{2,1,0:T(8,128)S(1)}, f32[6,28,896]{2,1,0:T(8,128)S(1)}) custom-call(bf16[1536,896]{1,0:T(8,128)(2,1)} %grad_ref.1, s32[1,32]{1,0:T(1,128)S(1)} %bitcast.1), custom_call_target="tpu_custom_call" | custom-call | tf_op jit(solution)/shard_map/stats/pallas_call | solution.py:521
  47.5 0.0 copy-done.2
  47.5 0.7 %multiply_add_fusion = f32[3,16,512]{2,1,0:T(8,128)} fusion(f32[3,16,512]{2,1,0:T(8,128)S(1)} %get-tuple-element.4, f32[3,16,512]{2,1,0:T(8,128)S(1)} %copy-done.2), kind=kLoop, calls=%fused_computation.1 | loop fusion | flops 49152 | bytes 294912 | tf_op jit(solution)/shard_map/add | solution.py:575
  48.1 0.0 copy-done.1
  48.1 0.9 %add_select_fusion = f32[6,28,896]{2,1,0:T(8,128)} fusion(f32[6,28,896]{2,1,0:T(8,128)S(1)} %get-tuple-element.5, f32[6,28,896]{2,1,0:T(8,128)S(1)} %copy-done.1), kind=kLoop, calls=%fused_computation | loop fusion | flops 602112 | bytes 1806336 | tf_op jit(solution)/shard_map/jit(_where)/select_n | solution.py:576
Async XLA Ops:
  0.6 0.7 %copy-start = (s32[32,1]{0,1:T(1,128)S(1)}, s32[32,1]{0,1:T(1,128)}, u32[]{:S(2)}) copy-start(s32[32,1]{0,1:T(1,128)} %param.5) | copy-start | bytes 388
  1.3 46.2 %copy-start.2 = (f32[3,16,512]{2,1,0:T(8,128)S(1)}, f32[3,16,512]{2,1,0:T(8,128)}, u32[]{:S(2)}) copy-start(f32[3,16,512]{2,1,0:T(8,128)} %param.6) | copy-start | bytes 294916
  1.3 46.9 %copy-start.1 = (f32[6,28,896]{2,1,0:T(8,128)S(1)}, f32[6,28,896]{2,1,0:T(8,128)}, u32[]{:S(2)}) copy-start(f32[6,28,896]{2,1,0:T(8,128)} %param.7) | copy-start | bytes 1806340
